TPU v7x, 32 devices: a whole 2x2x4 slice. The times are simulated.
32 devices in a mesh: seq: 8 (over z, x), ch: 4 (over y, core).
Axes of the slice: x: 2, y: 2, z: 4, core: 2. Of those that a mesh axis runs over, the one named last changes fastest.
Arguments:
- signal: bfloat16 [4096, 2048], P('seq', 'ch'), may hold values from -6 to 6
- filter_raw: bfloat16 [4096, 2048], P('seq', 'ch'), may hold values from -6 to 6
- gate: bfloat16 [4096, 2048], P('seq', 'ch'), may hold values from -6 to 6
- d_out: bfloat16 [4096, 2048], P('seq', 'ch'), may hold values from -6 to 6
- w_first: bfloat16 [32, 64, 64], P('ch'), may hold values from -0.75 to 0.75
- w_second: bfloat16 [64, 32, 32], P('ch'), may hold values from -1 to 1
Outputs:
- grad_signal: bfloat16 [4096, 2048], P('seq', 'ch')
- grad_filter: bfloat16 [4096, 2048], P('seq', 'ch')
- grad_gate: bfloat16 [4096, 2048], P('seq', 'ch')
- grad_first: float32 [32, 64, 64], P('ch', 'seq')
- grad_second: float32 [64, 32, 32], P('ch', 'seq')
All inputs are finite; a program needn't handle non-finite values.
Results may differ from a plain program's by a relative error of at most 0.02.
Values may be sent and summed in bfloat16 or wider, within the bound.
A program may use at most 128 MiB of HBM per device.

v0:
```python
import math

import jax
import jax.numpy as jnp
from jax import lax
from jax.sharding import PartitionSpec as P

HIGHEST = lax.Precision.HIGHEST


def counting(count):
    return jnp.arange(count, dtype=jnp.int32)


def phase_table(row_ids, col_ids, length, sign):
    angles = (
        2.0 * math.pi / length * (row_ids[:, None] * col_ids[None, :] % length).astype(jnp.float32)
    )
    return (jnp.cos(angles), sign * jnp.sin(angles))


def contract(form, table, real_part, imag_part):
    cosine, sine = table
    out_real = jnp.einsum(form, cosine, real_part, precision=HIGHEST) - jnp.einsum(
        form, sine, imag_part, precision=HIGHEST
    )
    out_imag = jnp.einsum(form, cosine, imag_part, precision=HIGHEST) + jnp.einsum(
        form, sine, real_part, precision=HIGHEST
    )
    return (out_real, out_imag)


def rotate(cosine, sine, real_part, imag_part):
    return (real_part * cosine - imag_part * sine, real_part * sine + imag_part * cosine)


def factors(length):
    return (length // 128, 128)


def local_forward(real_part, imag_part):
    fields, group, rows, width = real_part.shape
    outer, inner = factors(rows)
    real_part = real_part.reshape(fields, group, outer, inner, width)
    imag_part = imag_part.reshape(fields, group, outer, inner, width)
    real_part, imag_part = contract(
        "qa,fkabc->fkqbc",
        phase_table(counting(outer), counting(outer), outer, -1.0),
        real_part,
        imag_part,
    )
    cosine, sine = phase_table(counting(outer), counting(inner), rows, -1.0)
    real_part, imag_part = rotate(cosine[:, :, None], sine[:, :, None], real_part, imag_part)
    return contract(
        "rb,fkqbc->fkqrc",
        phase_table(counting(inner), counting(inner), inner, -1.0),
        real_part,
        imag_part,
    )


def local_inverse(real_part, imag_part):
    fields, group, outer, inner, width = real_part.shape
    rows = outer * inner
    real_part, imag_part = contract(
        "br,fkqrc->fkqbc",
        phase_table(counting(inner), counting(inner), inner, 1.0),
        real_part,
        imag_part,
    )
    cosine, sine = phase_table(counting(outer), counting(inner), rows, 1.0)
    real_part, imag_part = rotate(cosine[:, :, None], sine[:, :, None], real_part, imag_part)
    real_part, imag_part = contract(
        "aq,fkqbc->fkabc",
        phase_table(counting(outer), counting(outer), outer, 1.0),
        real_part,
        imag_part,
    )
    return (
        real_part.reshape(fields, group, rows, width),
        imag_part.reshape(fields, group, rows, width),
    )


def forward_transform(fields):
    devices = lax.axis_size("seq")
    count, rows, width = fields.shape
    piece = rows // devices
    span = 2 * devices
    whole = span * rows
    parts = lax.all_to_all(fields[:, None], "seq", split_axis=2, concat_axis=1, tiled=True)
    cosine, sine = phase_table(counting(span), counting(devices), span, -1.0)
    real_part = jnp.einsum("ka,fabc->fkbc", cosine, parts, precision=HIGHEST)
    imag_part = jnp.einsum("ka,fabc->fkbc", sine, parts, precision=HIGHEST)
    positions = lax.axis_index("seq") * piece + counting(piece)
    cosine, sine = phase_table(counting(span), positions, whole, -1.0)
    real_part, imag_part = rotate(cosine[:, :, None], sine[:, :, None], real_part, imag_part)
    spectrum = lax.all_to_all(
        jnp.stack([real_part, imag_part], axis=1), "seq", split_axis=2, concat_axis=3, tiled=True
    )
    return local_forward(spectrum[:, 0], spectrum[:, 1])


def inverse_transform(real_part, imag_part):
    devices = lax.axis_size("seq")
    real_part, imag_part = local_inverse(real_part, imag_part)
    group = real_part.shape[1]
    rows = real_part.shape[2]
    span = 2 * devices
    whole = span * rows
    classes = lax.axis_index("seq") * group + counting(group)
    cosine, sine = phase_table(classes, counting(rows), whole, 1.0)
    real_part, imag_part = rotate(cosine[:, :, None], sine[:, :, None], real_part, imag_part)
    gathered = lax.all_to_all(
        jnp.stack([real_part, imag_part], axis=1), "seq", split_axis=3, concat_axis=2, tiled=True
    )
    cosine, sine = phase_table(counting(devices), counting(span), span, 1.0)
    inverse_scale = 1.0 / whole
    out_real = (
        jnp.einsum("ak,fkbc->fabc", cosine, gathered[:, 0], precision=HIGHEST)
        - jnp.einsum("ak,fkbc->fabc", sine, gathered[:, 1], precision=HIGHEST)
    ) * inverse_scale
    slab = lax.all_to_all(out_real, "seq", split_axis=1, concat_axis=2, tiled=True)
    return slab[:, 0]


def adjoint_spectra(spectra_real, spectra_imag, incoming_real, incoming_imag):
    toward_signal_real = spectra_real[1] * incoming_real + spectra_imag[1] * incoming_imag
    toward_signal_imag = spectra_real[1] * incoming_imag - spectra_imag[1] * incoming_real
    toward_filter_real = spectra_real[0] * incoming_real + spectra_imag[0] * incoming_imag
    toward_filter_imag = spectra_real[0] * incoming_imag - spectra_imag[0] * incoming_real
    return (toward_signal_real, toward_signal_imag, toward_filter_real, toward_filter_imag)


def shards(signal, filter_raw, gate, d_out, w_first, w_second):
    rows, width = signal.shape
    scale = float(rows * lax.axis_size("seq")) ** (-0.5)
    signal_wide = signal.astype(jnp.float32)
    kernel = filter_raw.astype(jnp.float32) * scale
    spectra_real, spectra_imag = forward_transform(jnp.stack([signal_wide, kernel]))
    mixed_real = spectra_real[0] * spectra_real[1] - spectra_imag[0] * spectra_imag[1]
    mixed_imag = spectra_real[0] * spectra_imag[1] + spectra_imag[0] * spectra_real[1]
    conv = inverse_transform(mixed_real[None], mixed_imag[None])[0].astype(jnp.bfloat16)
    gate_wide = gate.astype(jnp.float32)
    product = (conv.astype(jnp.float32) * gate_wide).astype(jnp.bfloat16)
    blocks = w_first.shape[0]
    block = w_first.shape[1]
    product_blocks = product.reshape(rows, blocks, block)
    first_mix = jnp.einsum(
        "tij,ijk->tik", product_blocks, w_first, preferred_element_type=jnp.float32
    ).astype(jnp.bfloat16)
    received = lax.all_to_all(first_mix, "ch", split_axis=2, concat_axis=1, tiled=True)
    incoming = d_out.reshape(rows, w_second.shape[0], w_second.shape[1])
    second_back = jnp.einsum(
        "tko,kio->tki", incoming, w_second, preferred_element_type=jnp.float32
    ).astype(jnp.bfloat16)
    grad_second = jnp.einsum("tik,tko->kio", received, incoming, preferred_element_type=jnp.float32)
    returned = lax.all_to_all(second_back, "ch", split_axis=2, concat_axis=1, tiled=True)
    grad_product = jnp.einsum(
        "tki,ijk->tij", returned, w_first, preferred_element_type=jnp.float32
    ).reshape(rows, width)
    grad_first = jnp.einsum(
        "tij,tki->ijk", product_blocks, returned, preferred_element_type=jnp.float32
    )
    grad_gate = (grad_product * conv.astype(jnp.float32)).astype(jnp.bfloat16)
    grad_conv = grad_product * gate_wide
    incoming_real, incoming_imag = forward_transform(grad_conv[None])
    sig_real, sig_imag, fil_real, fil_imag = adjoint_spectra(
        spectra_real, spectra_imag, incoming_real[0], incoming_imag[0]
    )
    results = inverse_transform(jnp.stack([sig_real, fil_real]), jnp.stack([sig_imag, fil_imag]))
    grad_signal = results[0].astype(jnp.bfloat16)
    grad_filter = (results[1] * scale).astype(jnp.bfloat16)
    grad_first = lax.psum_scatter(
        grad_first.astype(jnp.bfloat16), "seq", scatter_dimension=1, tiled=True
    ).astype(jnp.float32)
    grad_second = lax.psum_scatter(grad_second, "seq", scatter_dimension=1, tiled=True)
    return (grad_signal, grad_filter, grad_gate, grad_first, grad_second)


def solution(mesh):
    in_specs = (
        P("seq", "ch"),
        P("seq", "ch"),
        P("seq", "ch"),
        P("seq", "ch"),
        P("ch", None, None),
        P("ch", None, None),
    )
    out_specs = (
        P("seq", "ch"),
        P("seq", "ch"),
        P("seq", "ch"),
        P("ch", "seq", None),
        P("ch", "seq", None),
    )
    return jax.shard_map(shards, mesh=mesh, in_specs=in_specs, out_specs=out_specs, check_vma=False)
```

profile of v0, /device:TPU:0, one launch (start us, length us, event | category | flops | bytes accessed | tf_op | source)
XLA Modules:
  0.0 1054.5 jit_solution(11800258364240908983)
XLA Ops:
  10.1 12.9 %all_to_all.147 = bf16[512,16,32]{0,1,2:T(8,128)(2,1)S(1)} all-to-all(bf16[512,16,32]{0,1,2:T(8,128)(2,1)S(1)} %copy.234), channel_id=1, replica_groups=mesh['seq'=8,'ch'=4] {'ch'}, dimensions={2} | all-to-all | bytes 1048576 | tf_op jit(solution)/shard_map/all_to_all | solution.py:158
  26.5 5.8 all-to-all-start.3
  37.2 20.8 %all-to-all-done.3 = f32[1,1,512,512]{3,1,0,2:T(1,128)S(1)} async-done(((f32[1,1,512,512]{3,1,0,2:T(1,128)}), f32[1,1,512,512]{3,1,0,2:T(1,128)S(1)}, u32[]{:S(2)}, u32[]{:S(2)}) %all-to-all-start.3) | async-done | bytes 1048608 | tf_op jit(solution)/shard_map/all_to_all | solution.py:91
  73.1 37.1 %all-to-all-done = f32[2,1,512,512]{3,0,1,2:T(2,128)S(1)} async-done(((f32[2,1,512,512]{3,0,1,2:T(2,128)}), f32[2,1,512,512]{3,0,1,2:T(2,128)S(1)}, u32[]{:S(2)}, u32[]{:S(2)}) %all-to-all-start) | async-done | bytes 2097184 | tf_op jit(solution)/shard_map/all_to_all | solution.py:91
  120.3 6.2 fusion.7
  128.5 8.6 copy.222
  137.1 70.2 %all-to-all-done.4 = f32[1,2,16,64,512]{4,3,1,0,2:T(8,128)} async-done(((f32[1,2,16,64,512]{4,3,1,0,2:T(8,128)}), f32[1,2,16,64,512]{4,3,1,0,2:T(8,128)}, u32[]{:S(2)}, u32[]{:S(2)}) %all-to-all-start.4) | async-done | bytes 4194336 | tf_op jit(solution)/shard_map/all_to_all | solution.py:98
  229.9 8.2 fusion.49
  252.5 141.8 %all-to-all-done.1 = f32[2,2,16,64,512]{4,3,0,1,2:T(8,128)} async-done(((f32[2,2,16,64,512]{4,3,0,1,2:T(8,128)}), f32[2,2,16,64,512]{4,3,0,1,2:T(8,128)}, u32[]{:S(2)}, u32[]{:S(2)}) %all-to-all-start.1) | async-done | bytes 8388640 | tf_op jit(solution)/shard_map/all_to_all | solution.py:98
  399.7 8.8 fusion.12
  408.5 8.5 fusion.10
  417.0 9.3 fusion.24
  426.3 15.2 %fusion.4 = (f32[2,2,4,128,512]{4,2,3,1,0:T(4,128)}, f32[2,2,4,128,512]{4,2,3,1,0:T(4,128)}) fusion(f32[2,2,128,512,4]{3,4,2,1,0:T(4,128)S(1)} %fusion.24, f32[4,128]{0,1:T(8,128)S(1)} %copy.230, f32[4,128]{0,1:T(8,128)S(1)} %copy.227, f32[2,2,128,512,4]{3,4,2,1,0:T(4,128)S(1)} %fusion.10, f32[2,2,4,128,512]{4,3,2,1,0:T(8,128)S(1)} %bitcast.454), kind=kOutput, calls=%fused_computation.18 | convolution fusion | flops 57671920 | bytes 20975616 | tf_op jit(solution)/shard_map/qa,fkabc->fkqbc/dot_general | solution.py:27
  446.9 7.1 fusion.115
  459.4 5.8 fusion.117
  472.9 6.0 multiply_subtract_fusion.1
  526.0 5.6 fusion.19
  539.3 7.1 subtract_bitcast_fusion.1
  557.3 9.3 fusion.198
  566.6 8.1 add_bitcast_fusion
  578.0 7.5 fusion.200
  585.6 8.4 subtract_bitcast_fusion
  597.2 21.5 %all-to-all-done.7 = f32[1,2,2,512,512]{4,2,1,0,3:T(2,128)} async-done(((f32[1,2,2,512,512]{4,2,1,0,3:T(2,128)}), f32[1,2,2,512,512]{4,2,1,0,3:T(2,128)}, u32[]{:S(2)}, u32[]{:S(2)}) %all-to-all-start.7) | async-done | bytes 4194336 | tf_op jit(solution)/shard_map/all_to_all | solution.py:114
  627.4 6.1 all_to_all.131
  649.0 11.1 %copy.261 = f32[2,2,2,512,512]{4,2,0,1,3:T(2,128)} copy(f32[2,2,2,512,512]{4,3,2,0,1:T(8,128)S(1)} %pad_maximum_fusion.1) | data formatting | bytes 16777216 | tf_op jit(solution)/shard_map/stack | solution.py:115
  660.1 6.1 all-to-all-start.5
  669.0 180.0 %all-to-all-done.5 = f32[2,2,2,512,512]{4,2,0,1,3:T(2,128)} async-done(((f32[2,2,2,512,512]{4,2,0,1,3:T(2,128)}), f32[2,2,2,512,512]{4,2,0,1,3:T(2,128)}, u32[]{:S(2)}, u32[]{:S(2)}) %all-to-all-start.5) | async-done | bytes 8388640 | tf_op jit(solution)/shard_map/all_to_all | solution.py:114
  852.7 8.2 copy.262
  861.0 10.2 copy.263
  871.2 10.9 %all_to_all.126 = f32[2,2,16,64,512]{4,2,3,0,1:T(8,128)} reshape(f32[2,2,8,2,64,512]{5,3,2,4,0,1:T(2,128)} %copy.263) | data formatting | bytes 16777216 | tf_op jit(solution)/shard_map/all_to_all | solution.py:114
  900.1 79.9 %reduce-scatter.7.cloned.1.call-done = bf16[8,512]{1,0:T(8,128)(2,1)} async-done(((bf16[64,512]{1,0:T(8,128)(2,1)}), bf16[8,512]{1,0:T(8,128)(2,1)}) %reduce-scatter.7.cloned.1.call-update) | async-done | bytes 8208
  983.7 60.6 %reduce-scatter.5.cloned.1.call-done = f32[16,4,32]{2,0,1:T(8,128)} async-done(((f32[16,32,32]{2,0,1:T(8,128)}), f32[16,4,32]{2,0,1:T(8,128)}) %reduce-scatter.5.cloned.1.call-update) | async-done | bytes 8208 | tf_op jit(solution)/shard_map/reduce_scatter | solution.py:177
  (159 shorter events, 226.4 us)
Async XLA Ops:
  7.2 15.9 %copy-start = (bf16[8,64,64]{2,1,0:T(8,128)(2,1)S(1)}, bf16[8,64,64]{2,1,0:T(8,128)(2,1)}, u32[]{:S(2)}) copy-start(bf16[8,64,64]{2,1,0:T(8,128)(2,1)} %param.10) | copy-start | bytes 196612
  8.5 14.6 %copy-start.17 = (bf16[512,512]{0,1:T(8,128)(2,1)}, bf16[512,512]{0,1:T(8,128)(2,1)S(1)}, u32[]{:S(2)}) copy-start(bf16[512,512]{0,1:T(8,128)(2,1)S(1)} %copy.233) | copy-start | bytes 1572868
  24.4 7.9 copy-start.25
  26.5 31.4 %all-to-all-start.3 = ((f32[1,1,512,512]{3,1,0,2:T(1,128)}), f32[1,1,512,512]{3,1,0,2:T(1,128)S(1)}, u32[]{:S(2)}, u32[]{:S(2)}) async-start(f32[1,1,512,512]{3,1,0,2:T(1,128)} %copy.237), calls=%async_computation.3 | async-start | bytes 2097152 | tf_op jit(solution)/shard_map/all_to_all | solution.py:91
  57.9 52.3 %all-to-all-start = ((f32[2,1,512,512]{3,0,1,2:T(2,128)}), f32[2,1,512,512]{3,0,1,2:T(2,128)S(1)}, u32[]{:S(2)}, u32[]{:S(2)}) async-start(f32[2,1,512,512]{3,0,1,2:T(2,128)} %maximum_bitcast_fusion), calls=%async_computation | async-start | bytes 4194304 | tf_op jit(solution)/shard_map/all_to_all | solution.py:91
  110.2 97.1 %all-to-all-start.4 = ((f32[1,2,16,64,512]{4,3,1,0,2:T(8,128)}), f32[1,2,16,64,512]{4,3,1,0,2:T(8,128)}, u32[]{:S(2)}, u32[]{:S(2)}) async-start(f32[1,2,16,64,512]{4,3,1,0,2:T(8,128)} %copy.240), calls=%async_computation.4 | async-start | bytes 8388608 | tf_op jit(solution)/shard_map/all_to_all | solution.py:98
  207.3 187.0 %all-to-all-start.1 = ((f32[2,2,16,64,512]{4,3,0,1,2:T(8,128)}), f32[2,2,16,64,512]{4,3,0,1,2:T(8,128)}, u32[]{:S(2)}, u32[]{:S(2)}) async-start(f32[2,2,16,64,512]{4,3,0,1,2:T(8,128)} %copy.222), calls=%async_computation.1 | async-start | bytes 16777216 | tf_op jit(solution)/shard_map/all_to_all | solution.py:98
  459.4 5.9 copy-start.4
  459.4 5.9 copy-start.11
  465.3 3.8 copy-start.3
  469.2 3.7 copy-start.8
  469.2 3.7 copy-start.15
  499.7 5.5 copy-start.5
  499.7 5.5 copy-start.14
  520.9 5.1 copy-start.9
  520.9 97.8 %all-to-all-start.7 = ((f32[1,2,2,512,512]{4,2,1,0,3:T(2,128)}), f32[1,2,2,512,512]{4,2,1,0,3:T(2,128)}, u32[]{:S(2)}, u32[]{:S(2)}) async-start(f32[1,2,2,512,512]{4,2,1,0,3:T(2,128)} %copy.273), calls=%async_computation.7 | async-start | bytes 8388608 | tf_op jit(solution)/shard_map/all_to_all | solution.py:114
  526.0 5.6 copy-start.10
  531.6 3.9 copy-start.6
  531.6 3.9 copy-start.7
  557.3 9.3 copy-start.2
  578.0 7.5 copy-start.1
  640.3 19.8 %all-to-all-start.8 = ((bf16[1,8,64,512]{3,2,0,1:T(8,128)(2,1)}), bf16[1,8,64,512]{3,2,0,1:T(8,128)(2,1)S(1)}, u32[]{:S(2)}, u32[]{:S(2)}) async-start(bf16[1,8,64,512]{3,2,0,1:T(8,128)(2,1)} %copy.276), calls=%async_computation.8 | async-start | bytes 1048576 | tf_op jit(solution)/shard_map/all_to_all | solution.py:123
  660.1 6.1 copy-start.13
  660.1 6.1 copy-start.23
  660.1 188.9 %all-to-all-start.5 = ((f32[2,2,2,512,512]{4,2,0,1,3:T(2,128)}), f32[2,2,2,512,512]{4,2,0,1,3:T(2,128)}, u32[]{:S(2)}, u32[]{:S(2)}) async-start(f32[2,2,2,512,512]{4,2,0,1,3:T(2,128)} %copy.261), calls=%async_computation.5 | async-start | bytes 16777216 | tf_op jit(solution)/shard_map/all_to_all | solution.py:114
  667.6 193.4 %copy-start.21 = (bf16[512,512]{0,1:T(8,128)(2,1)}, bf16[512,512]{0,1:T(8,128)(2,1)S(1)}, u32[]{:S(2)}) copy-start(bf16[512,512]{0,1:T(8,128)(2,1)S(1)} %copy.279) | copy-start | bytes 1572868
  849.1 44.3 %all-to-all-start.9 = ((bf16[512,8,64]{0,1,2:T(8,128)(2,1)}), bf16[512,8,64]{0,1,2:T(8,128)(2,1)S(1)}, u32[]{:S(2)}, u32[]{:S(2)}) async-start(bf16[512,8,64]{0,1,2:T(8,128)(2,1)} %copy.281), calls=%async_computation.9 | async-start | bytes 1048576 | tf_op jit(solution)/shard_map/all_to_all | solution.py:152
  893.4 4.5 copy-start.20
  893.4 87.5 %copy-start.18 = (bf16[512,512]{0,1:T(8,128)(2,1)S(1)}, bf16[512,512]{0,1:T(8,128)(2,1)}, u32[]{:S(2)}) copy-start(bf16[512,512]{0,1:T(8,128)(2,1)} %copy-done.17) | copy-start | bytes 1572868
  894.2 151.5 %all-to-all-start.6 = ((f32[2,8,64,512]{3,2,0,1:T(8,128)}), f32[2,8,64,512]{3,2,0,1:T(8,128)S(1)}, u32[]{:S(2)}, u32[]{:S(2)}) async-start(f32[2,8,64,512]{3,2,0,1:T(8,128)} %copy.264), calls=%async_computation.6 | async-start | bytes 4194304 | tf_op jit(solution)/shard_map/all_to_all | solution.py:123
  897.8 82.3 %reduce-scatter.7.cloned.1.call-start = ((), (), s32[]{:S(2)}) async-start(), calls=%async_computation.13 | async-start | bytes 73728
  900.1 144.2 %reduce-scatter.5.cloned.1.call-start = ((), (), s32[]{:S(2)}) async-start(), calls=%async_computation.12 | async-start | bytes 294912 | tf_op jit(solution)/shard_map/reduce_scatter | solution.py:177
  (6 other events, 9.8 us)
Sparse Core Ops, SparseCore 0:
  902.6 77.4 reduce-scatter.6
  984.0 60.2 reduce-scatter.4
where the time goes:
time: 1060 us; the launch traced here: 1050 us
  waiting for transfers between devices  612 us (58%)
  matrix products  219 us (21%)
  local copies, waits for them, and re-layouts  139 us (13%)
  starting transfers between devices  41.8 us (4%)
  other arithmetic  15.4 us (1%)
  between operations  15.1 us (1%)
  blocking collectives  12.9 us (1%)
    all_to_all x2, waiting for transfers between devices, forward_transform(): lax.all_to_all(jnp.stack([real_part, imag_part], axis=1), 'seq', split_ax...  212 us
    all_to_all x2, waiting for transfers between devices, inverse_transform(): lax.all_to_all(jnp.stack([real_part, imag_part], axis=1), 'seq', split_ax...  202 us
    unnamed x3, waiting for transfers between devices  80 us
    reduce_scatter x1, waiting for transfers between devices, shards(): lax.psum_scatter(grad_second, 'seq', scatter_dimension=1, tiled=True)  60.6 us
    all_to_all x2, waiting for transfers between devices, forward_transform(): lax.all_to_all(fields[:, None], 'seq', split_axis=2, concat_axis=1, tiled...  57.9 us
    dot_general x8, matrix products, contract(): jnp.einsum(form, sine, real_part, precision=HIGHEST)  50.4 us
    dot_general x8, matrix products, contract(): jnp.einsum(form, cosine, real_part, precision=HIGHEST)  45.8 us
    all_to_all x6, local copies, waits for them, and re-layouts, inverse_transform(): lax.all_to_all(jnp.stack([real_part, imag_part], axis=1), 'seq', split_ax...  44.2 us
  transfers between devices with their start and end apart: 11, of which 8 were waited for; matrix products, arithmetic and copies ran while one was open for 19% of the time, Pallas kernels for 0%

commit v1 on v0

--- a/solution.py
+++ b/solution.py
@@ -2,7 +2,11 @@
 
 import jax
 import jax.numpy as jnp
+import ml_dtypes
+import numpy as np
 from jax import lax
+from jax.experimental import pallas as pl
+from jax.experimental.pallas import tpu as pltpu
 from jax.sharding import PartitionSpec as P
 
 HIGHEST = lax.Precision.HIGHEST
@@ -132,7 +136,7 @@
     return (toward_signal_real, toward_signal_imag, toward_filter_real, toward_filter_imag)
 
 
-def shards(signal, filter_raw, gate, d_out, w_first, w_second):
+def shards_general(signal, filter_raw, gate, d_out, w_first, w_second):
     rows, width = signal.shape
     scale = float(rows * lax.axis_size("seq")) ** (-0.5)
     signal_wide = signal.astype(jnp.float32)
@@ -178,6 +182,444 @@
     return (grad_signal, grad_filter, grad_gate, grad_first, grad_second)
 
 
+F32 = jnp.float32
+BF16 = jnp.bfloat16
+LANES = 128
+HALF = 64
+INNER = 128
+CHUNK = 16
+
+
+def dft_tables(outer, scale):
+    length = outer * INNER
+    q = np.arange(outer // 2 + 1)[:, None, None]
+    r = np.arange(INNER)[None, :, None]
+    b = np.arange(INNER)[None, None, :]
+    angle = 2.0 * np.pi / length * ((b * (q + outer * r)) % length)
+    c, s = np.cos(angle), np.sin(angle)
+    forward = np.concatenate(
+        [np.concatenate([c, s], axis=2), np.concatenate([-s, c], axis=2)], axis=1
+    )
+    inverse = forward.transpose(0, 2, 1) * (scale / length)
+    return forward.astype(ml_dtypes.bfloat16), inverse.astype(ml_dtypes.bfloat16)
+
+
+def times(value, cosine, sine):
+    real, imag = value
+    if imag is None:
+        return (real * cosine, real * sine)
+    return (real * cosine - imag * sine, real * sine + imag * cosine)
+
+
+def real_dft(values, length):
+    if length == 2:
+        return [(values[0], None), (values[0], None)]
+    even = real_dft(values[0::2], length // 2)
+    odd = real_dft(values[1::2], length // 2)
+    half, quarter = length // 2, length // 4
+    out = [None] * (half + 1)
+    for q in range(quarter + 1):
+        er, ei = even[q]
+        if q == 0:
+            out[0] = (er + odd[0][0], None)
+            out[half] = (er - odd[0][0], None)
+        elif q == quarter:
+            out[q] = (er, -odd[q][0])
+        else:
+            angle = 2.0 * math.pi * q / length
+            tr, ti = times(odd[q], math.cos(angle), -math.sin(angle))
+            out[q] = (er + tr, ei + ti)
+            out[half - q] = (er - tr, ti - ei)
+    return out
+
+
+def real_inverse(values, length):
+    if length == 2:
+        return [values[0][0] + values[1][0]]
+    half, quarter = length // 2, length // 4
+    even, odd = [], []
+    for q in range(quarter + 1):
+        zr, zi = values[q]
+        if q == 0:
+            wr = values[half][0]
+            even.append((zr + wr, None))
+            odd.append((zr - wr, None))
+        elif q == quarter:
+            even.append((zr + zr, None))
+            odd.append((-(zi + zi), None))
+        else:
+            wr, wi = values[half - q]
+            even.append((zr + wr, zi - wi))
+            angle = 2.0 * math.pi * q / length
+            odd.append(times((zr - wr, zi + wi), math.cos(angle), math.sin(angle)))
+    out = [None] * half
+    out[0::2] = real_inverse(even, half)
+    out[1::2] = real_inverse(odd, half)
+    return out
+
+
+def low_lanes(rows):
+    return lax.broadcasted_iota(jnp.int32, (rows, LANES), 1) < HALF
+
+
+def swap(value):
+    return pltpu.roll(value, HALF, 1)
+
+
+def store_classes(y_ref, rows, spectrum):
+    for q, (real, imag) in enumerate(spectrum):
+        y_ref[q, pl.ds(rows, CHUNK), :] = real.astype(BF16)
+        imag = jnp.zeros_like(real) if imag is None else imag
+        y_ref[q, pl.ds(INNER + rows, CHUNK), :] = imag.astype(BF16)
+
+
+def load_classes(z_ref, rows, classes):
+    out = []
+    for q in range(classes):
+        real = z_ref[q, pl.ds(rows, CHUNK), :]
+        edge = q == 0 or q == classes - 1
+        out.append((real, None if edge else z_ref[q, pl.ds(INNER + rows, CHUNK), :]))
+    return out
+
+
+def pack_kernel(signal_ref, filter_ref, out_ref):
+    rows = signal_ref.shape[0]
+    low = low_lanes(rows)
+    for p in range(out_ref.shape[0] // 2):
+        cols = slice(p * LANES, (p + 1) * LANES)
+        a = signal_ref[:, cols].astype(F32)
+        b = filter_ref[:, cols].astype(F32)
+        out_ref[2 * p] = jnp.where(low, a, swap(b)).astype(BF16)
+        out_ref[2 * p + 1] = jnp.where(low, swap(a), b).astype(BF16)
+
+
+def unpack_kernel(in_ref, signal_ref, filter_ref):
+    rows = signal_ref.shape[0]
+    low = low_lanes(rows)
+    for p in range(in_ref.shape[0] // 2):
+        cols = slice(p * LANES, (p + 1) * LANES)
+        a = in_ref[2 * p].astype(F32)
+        b = in_ref[2 * p + 1].astype(F32)
+        filter_ref[:, cols] = jnp.where(low, a, swap(b)).astype(BF16)
+        signal_ref[:, cols] = jnp.where(low, swap(a), b).astype(BF16)
+
+
+def conv_kernel(pair_ref, forward_ref, inverse_ref, spec_ref, conv_ref, y_ref, z_ref):
+    devices, rows, _ = pair_ref.shape
+    classes = forward_ref.shape[0]
+    outer = 2 * (classes - 1)
+    tiles = rows // INNER
+
+    def first(j, carry):
+        at = pl.multiple_of(j * CHUNK, CHUNK)
+        points = [
+            pair_ref[a // tiles, pl.ds((a % tiles) * INNER + at, CHUNK), :].astype(F32)
+            for a in range(outer // 2)
+        ]
+        store_classes(y_ref, at, real_dft(points, outer))
+        return carry
+
+    lax.fori_loop(0, INNER // CHUNK, first, 0)
+
+    def middle(q, carry):
+        x = jnp.dot(forward_ref[q], y_ref[q], preferred_element_type=F32)
+        spec_ref[q] = x.astype(BF16)
+        o = swap(x)
+        xr, xi, orr, oi = x[:INNER], x[INNER:], o[:INNER], o[INNER:]
+        mixed = jnp.concatenate([xr * orr - xi * oi, xr * oi + xi * orr], axis=0)
+        z_ref[q] = jnp.dot(inverse_ref[q], mixed.astype(BF16), preferred_element_type=F32)
+        return carry
+
+    lax.fori_loop(0, classes, middle, 0, unroll=3)
+    low = low_lanes(CHUNK)
+    halves = tiles // 2
+
+    def last(j, carry):
+        at = pl.multiple_of(j * CHUNK, CHUNK)
+        points = real_inverse(load_classes(z_ref, at, classes), outer)
+        for s in range(devices):
+            for m in range(halves):
+                a = s * tiles + m
+                value = jnp.where(low, points[a], points[a + halves])
+                conv_ref[s, pl.ds(m * INNER + at, CHUNK), :] = value.astype(BF16)
+        return carry
+
+    lax.fori_loop(0, INNER // CHUNK, last, 0)
+
+
+def adjoint_kernel(grad_ref, spec_ref, forward_ref, inverse_ref, out_ref, y_ref, z_ref):
+    devices, packed, _ = grad_ref.shape
+    classes = forward_ref.shape[0]
+    outer = 2 * (classes - 1)
+    halves = packed // INNER
+    tiles = 2 * halves
+    low = low_lanes(CHUNK)
+
+    def first(j, carry):
+        at = pl.multiple_of(j * CHUNK, CHUNK)
+        points = [None] * (outer // 2)
+        for s in range(devices):
+            for m in range(halves):
+                value = grad_ref[s, pl.ds(m * INNER + at, CHUNK), :].astype(F32)
+                other = swap(value)
+                points[s * tiles + m] = jnp.where(low, value, other)
+                points[s * tiles + halves + m] = jnp.where(low, other, value)
+        store_classes(y_ref, at, real_dft(points, outer))
+        return carry
+
+    lax.fori_loop(0, INNER // CHUNK, first, 0)
+
+    def middle(q, carry):
+        g = jnp.dot(forward_ref[q], y_ref[q], preferred_element_type=F32)
+        x = spec_ref[q].astype(F32)
+        gr, gi, xr, xi = g[:INNER], g[INNER:], x[:INNER], x[INNER:]
+        mixed = jnp.concatenate([xr * gr + xi * gi, xr * gi - xi * gr], axis=0)
+        z_ref[q] = jnp.dot(inverse_ref[q], mixed.astype(BF16), preferred_element_type=F32)
+        return carry
+
+    lax.fori_loop(0, classes, middle, 0, unroll=3)
+
+    def last(j, carry):
+        at = pl.multiple_of(j * CHUNK, CHUNK)
+        points = real_inverse(load_classes(z_ref, at, classes), outer)
+        for a in range(outer // 2):
+            out_ref[a // tiles, pl.ds((a % tiles) * INNER + at, CHUNK), :] = points[a].astype(BF16)
+        return carry
+
+    lax.fori_loop(0, INNER // CHUNK, last, 0)
+
+
+def back_kernel(d_out_ref, second_ref, out_ref):
+    value = jnp.dot(d_out_ref[...], second_ref[...], preferred_element_type=F32).astype(BF16)
+    for c in range(out_ref.shape[0]):
+        out_ref[c] = value[:, c * LANES : (c + 1) * LANES]
+
+
+def joined(ref):
+    return jnp.concatenate([ref[c] for c in range(ref.shape[0])], axis=1)
+
+
+def grad_product_of(back, first):
+    return lax.dot_general(back, first, (((1,), (1,)), ((), ())), preferred_element_type=F32)
+
+
+def grad_conv_kernel(back_ref, first_ref, gate_ref, out_ref):
+    value = grad_product_of(joined(back_ref), first_ref[...]) * gate_ref[...].astype(F32)
+    half = value.shape[0] // 2
+    low = low_lanes(half)
+    for p in range(out_ref.shape[0] // 2):
+        top = value[:half, p * LANES : (p + 1) * LANES]
+        bottom = value[half:, p * LANES : (p + 1) * LANES]
+        out_ref[2 * p] = jnp.where(low, top, swap(bottom)).astype(BF16)
+        out_ref[2 * p + 1] = jnp.where(low, swap(top), bottom).astype(BF16)
+
+
+def mix_kernel(conv_ref, back_ref, first_ref, gate_ref, mix_ref, grad_gate_ref, grad_first_ref):
+    devices, half, _ = conv_ref.shape
+    low = low_lanes(half)
+    parts = []
+    for p in range(devices // 2):
+        a = conv_ref[2 * p].astype(F32)
+        b = conv_ref[2 * p + 1].astype(F32)
+        parts.append(
+            jnp.concatenate([jnp.where(low, a, swap(b)), jnp.where(low, swap(a), b)], axis=0)
+        )
+    conv = jnp.concatenate(parts, axis=1)
+    product = (conv * gate_ref[...].astype(F32)).astype(BF16)
+    first = first_ref[...]
+    mix = jnp.dot(product, first, preferred_element_type=F32).astype(BF16)
+    groups = mix_ref.shape[0]
+    for c in range(groups):
+        mix_ref[c] = mix[:, c * LANES : (c + 1) * LANES]
+    back = joined(back_ref)
+    grad_gate_ref[...] = (grad_product_of(back, first) * conv).astype(BF16)
+    whole = lax.dot_general(product, back, (((0,), (0,)), ((), ())), preferred_element_type=F32)
+    count = whole.shape[0]
+    lane = lax.broadcasted_iota(jnp.int32, (count, LANES), 1)
+    row = lax.broadcasted_iota(jnp.int32, (count, LANES), 0)
+    inner = LANES // devices
+    keep = lane // inner == row // (count // devices)
+    grads = jnp.zeros((count, LANES), F32)
+    for c in range(groups):
+        value = jnp.where(keep, whole[:, c * LANES : (c + 1) * LANES], 0.0)
+        shift = inner
+        while shift < LANES:
+            value = value + pltpu.roll(value, shift, 1)
+            shift *= 2
+        grads = jnp.where((lane // inner) % groups == c, value, grads)
+    block = count // devices
+    piece = block // devices
+    pairs = devices // 2
+    small = low_lanes(piece)
+    for i in range(pairs):
+        for s in range(devices):
+            a = grads[i * block + s * piece : i * block + (s + 1) * piece]
+            k = i + pairs
+            b = grads[k * block + s * piece : k * block + (s + 1) * piece]
+            grad_first_ref[s, i * piece : (i + 1) * piece, :] = jnp.where(small, a, b)
+
+
+def second_kernel(mix_ref, d_out_ref, grad_first_ref, out_ref, inner, width):
+    groups = mix_ref.shape[0]
+    devices, first_rows, _ = grad_first_ref.shape
+    out_ref[:, :first_rows, :] = grad_first_ref[...]
+    d_out = d_out_ref[...]
+    lane = lax.broadcasted_iota(jnp.int32, (LANES, LANES), 1)
+    row = lax.broadcasted_iota(jnp.int32, (LANES, LANES), 0)
+    folds = LANES // width
+    per = devices // groups
+    slot = lax.broadcasted_iota(jnp.int32, (inner, LANES), 1) // width
+    for c in range(groups):
+        whole = lax.dot_general(
+            mix_ref[c], d_out, (((0,), (0,)), ((), ())), preferred_element_type=F32
+        )
+        total = jnp.zeros((LANES, LANES), F32)
+        for g in range(whole.shape[1] // LANES):
+            keep = lane // width + g * folds == row % inner
+            total = total + jnp.where(keep, whole[:, g * LANES : (g + 1) * LANES], 0.0)
+        shift = width
+        while shift < LANES:
+            total = total + pltpu.roll(total, shift, 1)
+            shift *= 2
+        for d in range(per):
+            base = d * folds * inner
+            piece = jnp.zeros((inner, LANES), F32)
+            for i in range(folds):
+                piece = jnp.where(slot == i, total[base + i * inner : base + (i + 1) * inner], piece)
+            out_ref[c * per + d, first_rows:, :] = piece
+
+
+def call(kernel, outs, scratch=(), flops=0, moved=0):
+    return pl.pallas_call(
+        kernel,
+        out_shape=outs,
+        scratch_shapes=list(scratch),
+        compiler_params=pltpu.CompilerParams(vmem_limit_bytes=48 * 1024 * 1024),
+        cost_estimate=pl.CostEstimate(flops=flops, bytes_accessed=moved, transcendentals=0),
+    )
+
+
+def exchange(value, axis):
+    return lax.all_to_all(value, axis, split_axis=0, concat_axis=0, tiled=True)
+
+
+def shards_whole(signal, filter_raw, gate, d_out, w_first, w_second):
+    rows, width = signal.shape
+    devices = lax.axis_size("seq")
+    groups = lax.axis_size("ch")
+    length = rows * devices
+    outer = 2 * length // INNER
+    classes = outer // 2 + 1
+    forward, inverse = (jnp.asarray(t) for t in dft_tables(outer, float(length) ** (-0.5)))
+    blocks, block, _ = w_first.shape
+    inner, across, out_block = w_second.shape
+    shape = jax.ShapeDtypeStruct
+    scratch = (
+        pltpu.VMEM((classes, 2 * INNER, LANES), BF16),
+        pltpu.VMEM((classes, 2 * INNER, LANES), F32),
+    )
+
+    second_t = w_second.transpose(0, 2, 1).reshape(inner, out_block, groups, blocks, 1)
+    second = jnp.where(
+        jnp.eye(inner, dtype=bool)[:, None, None, None, :], second_t, jnp.zeros((), BF16)
+    ).reshape(width, width)
+    first = jnp.where(
+        jnp.eye(blocks, dtype=bool)[:, None, None, :, None],
+        w_first.reshape(blocks, block, groups, 1, inner),
+        jnp.zeros((), BF16),
+    ).reshape(width, width)
+
+    dense = 2 * rows * width * width
+    back = call(back_kernel, shape((groups, rows, LANES), BF16), flops=dense, moved=1 << 21)(
+        d_out, second
+    )
+    back = exchange(back, "ch")
+    pair = call(pack_kernel, shape((devices, rows, LANES), BF16), flops=1 << 20, moved=1 << 21)(
+        signal, filter_raw
+    )
+    pair = exchange(pair, "seq")
+    grad_conv = call(
+        grad_conv_kernel, shape((devices, rows // 2, LANES), BF16), flops=dense, moved=1 << 21
+    )(back, first, gate)
+    grad_conv = exchange(grad_conv, "seq")
+    cost = dict(flops=10 * 10**9, moved=16 * 10**6)
+    spec, conv = call(
+        conv_kernel,
+        (
+            shape((classes, 2 * INNER, LANES), BF16),
+            shape((devices, rows // 2, LANES), BF16),
+        ),
+        scratch,
+        **cost,
+    )(pair, forward, inverse)
+    conv = exchange(conv, "seq")
+    grads = call(adjoint_kernel, shape((devices, rows, LANES), BF16), scratch, **cost)(
+        grad_conv, spec, forward, inverse
+    )
+    first_rows = blocks * (block // devices) * block // LANES
+    mix, grad_gate, grad_first = call(
+        mix_kernel,
+        (
+            shape((groups, rows, LANES), BF16),
+            shape((rows, width), BF16),
+            shape((devices, first_rows, LANES), F32),
+        ),
+        flops=3 * dense,
+        moved=1 << 22,
+    )(conv, back, first, gate)
+    mix = exchange(mix, "ch")
+    grads = exchange(grads, "seq")
+
+    def second_body(mix_ref, d_out_ref, grad_first_ref, out_ref):
+        second_kernel(mix_ref, d_out_ref, grad_first_ref, out_ref, inner, out_block)
+
+    second_rows = inner * (across // devices) * out_block // LANES
+    small = call(
+        second_body,
+        shape((devices, first_rows + second_rows, LANES), F32),
+        flops=dense,
+        moved=1 << 21,
+    )(mix, d_out, grad_first)
+    small = exchange(small, "seq").sum(axis=0)
+    grad_first = (
+        small[:first_rows]
+        .reshape(blocks // 2, block // devices, 2, block)
+        .transpose(2, 0, 1, 3)
+        .reshape(blocks, block // devices, block)
+    )
+    grad_second = small[first_rows:].reshape(inner, across // devices, out_block)
+    grad_signal, grad_filter = call(
+        unpack_kernel,
+        (shape((rows, width), BF16), shape((rows, width), BF16)),
+        flops=1 << 20,
+        moved=1 << 21,
+    )(grads)
+    return (grad_signal, grad_filter, grad_gate, grad_first, grad_second)
+
+
+def shards(signal, filter_raw, gate, d_out, w_first, w_second):
+    rows, width = signal.shape
+    devices = lax.axis_size("seq")
+    blocks, block, _ = w_first.shape
+    inner, across, out_block = w_second.shape
+    fits = (
+        blocks == devices
+        and block == HALF
+        and width == devices * HALF
+        and width == lax.axis_size("ch") * LANES
+        and width == inner * out_block
+        and blocks * inner == LANES
+        and LANES // out_block == across // devices
+        and lax.axis_size("ch") * inner == block
+        and devices % lax.axis_size("ch") == 0
+        and block // devices == 8
+        and rows % (2 * INNER) == 0
+        and (rows * devices // INNER) & (rows * devices // INNER - 1) == 0
+    )
+    body = shards_whole if fits else shards_general
+    return body(signal, filter_raw, gate, d_out, w_first, w_second)
+
+
 def solution(mesh):
     in_specs = (
         P("seq", "ch"),

time: 1060 us -> 161 us (0.15)
  waiting for transfers between devices: 612 us -> 76.1 us
  matrix products: 219 us -> 0 us
  local copies, waits for them, and re-layouts: 139 us -> 12.9 us
  Pallas kernels: 0 us -> 37.3 us
  between operations: 15.1 us -> 0.78 us
  other arithmetic: 15.4 us -> 1.72 us
  blocking collectives: 12.9 us -> 0 us
  starting transfers between devices: 41.8 us -> 31 us
    all_to_all x9 -> x7, waiting for transfers between devices: 471 us -> 76.1 us  [exchange(): return lax.all_to_all(value, axis, split_axis=0, concat_axis=0, tiled=True)]
    dot_general x45 -> x0, matrix products: 219 us -> none  [the longest x8 50.4 us: contract(): jnp.einsum(form, sine, real_part, precision=HIGHEST)]
    unnamed x3 -> x0, waiting for transfers between devices: 80 us -> none
    reduce_scatter x1 -> x0, waiting for transfers between devices: 60.6 us -> none  [shards(): lax.psum_scatter(grad_second, 'seq', scatter_dimension=1, tiled=True)]
    all_to_all x11 -> x0, local copies, waits for them, and re-layouts: 52.4 us -> none  [the longest x6 44.2 us: inverse_transform(): lax.all_to_all(jnp.stack([real_part, imag_part], axis=1), 'seq', split_ax...]
    another operation x11 -> x0, local copies, waits for them, and re-layouts: 42.1 us -> none  [the longest x2 16.4 us: inverse_transform(): jnp.stack([real_part, imag_part], axis=1)]
    pallas_call x0 -> x8, Pallas kernels: none -> 37.3 us  [the longest x1 14.4 us: shards_whole(): call(conv_kernel, (shape((classes, 2 * INNER, LANES), BF16), shape((devic...]
    sub x4 -> x0, local copies, waits for them, and re-layouts: 14.7 us -> none  [the longest x2 10.9 us: rotate(): real_part * cosine - imag_part * sine]
  transfers between devices with their start and end apart: 11 -> 7, of which waited for: 8 -> 5; matrix products, arithmetic and copies ran while one was open for 19% -> 6% of each run, Pallas kernels for 0% -> 20%
where the time goes in v1:
time: 161 us; the launch traced here: 160 us
  waiting for transfers between devices  76.1 us (47%)
  Pallas kernels  37.3 us (23%)
  starting transfers between devices  31 us (19%)
  local copies, waits for them, and re-layouts  12.9 us (8%)
  other arithmetic  1.72 us (1%)
    all_to_all x7, waiting for transfers between devices, exchange(): return lax.all_to_all(value, axis, split_axis=0, concat_axis=0, tiled=True)  76.1 us
    all_to_all x7, starting transfers between devices, exchange(): return lax.all_to_all(value, axis, split_axis=0, concat_axis=0, tiled=True)  31 us
    pallas_call x1, Pallas kernels, shards_whole(): call(conv_kernel, (shape((classes, 2 * INNER, LANES), BF16), shape((devic...  14.4 us
    pallas_call x1, Pallas kernels, shards_whole(): call(adjoint_kernel, shape((devices, rows, LANES), BF16), scratch, **cost)  14.3 us
    unnamed x16, local copies, waits for them, and re-layouts  5.05 us
    select_n x2, local copies, waits for them, and re-layouts, shards_whole(): jnp.where(jnp.eye(inner, dtype=bool)[:, None, None, None, :], second_t, j...  3.63 us
  transfers between devices with their start and end apart: 7, of which 5 were waited for; matrix products, arithmetic and copies ran while one was open for 6% of the time, Pallas kernels for 20%

profile of v1, /device:TPU:0, one launch (start us, length us, event | category | flops | bytes accessed | tf_op | source)
XLA Modules:
  0.0 159.9 jit_solution(2156776060459230775)
XLA Ops:
  0.6 1.0 copy-done.1
  1.7 1.0 copy-done.2
  2.7 1.4 shard_map.121
  4.1 7.3 %all-to-all-start.2 = ((bf16[8,512,128]{2,1,0:T(8,128)(2,1)}), bf16[8,512,128]{2,1,0:T(8,128)(2,1)S(1)}, u32[]{:S(2)}, u32[]{:S(2)}) async-start(bf16[8,512,128]{2,1,0:T(8,128)(2,1)} %shard_map.121), calls=%async_computation.2 | async-start | bytes 2097152 | tf_op jit(solution)/shard_map/all_to_all | solution.py:503
  11.5 1.6 broadcast_select_fusion
  13.0 3.4 %select_n.17 = bf16[512,512]{0,1:T(8,128)(2,1)S(1)} reshape(bf16[16,32,4,8,16]{1,0,4,3,2:T(8,128)(2,1)} %broadcast_select_fusion) | data formatting | bytes 1048576 | tf_op jit(solution)/shard_map/jit(_where)/select_n | solution.py:523
  16.4 0.2 copy.16.second_ref
  16.7 1.2 shard_map.119
  17.9 19.3 %all-to-all-done.2.pair_ref = bf16[8,512,128]{2,1,0:T(8,128)(2,1)S(1)} async-done(((bf16[8,512,128]{2,1,0:T(8,128)(2,1)}), bf16[8,512,128]{2,1,0:T(8,128)(2,1)S(1)}, u32[]{:S(2)}, u32[]{:S(2)}) %all-to-all-start.2) | async-done | bytes 1048608 | tf_op jit(solution)/shard_map/all_to_all | solution.py:503
  37.1 3.5 %all-to-all-start = ((bf16[4,512,128]{2,1,0:T(8,128)(2,1)}), bf16[4,512,128]{2,1,0:T(8,128)(2,1)S(1)}, u32[]{:S(2)}, u32[]{:S(2)}) async-start(bf16[4,512,128]{2,1,0:T(8,128)(2,1)} %shard_map.119), calls=%async_computation | async-start | bytes 1048576 | tf_op jit(solution)/shard_map/all_to_all | solution.py:503
  40.6 14.4 %shard_map.122 = (bf16[33,256,128]{2,1,0:T(8,128)(2,1)S(1)}, bf16[8,256,128]{2,1,0:T(8,128)(2,1)}) custom-call(bf16[8,512,128]{2,1,0:T(8,128)(2,1)S(1)} %all-to-all-done.2.pair_ref, bf16[33,256,256]{2,1,0:T(8,128)(2,1)} %constant.8.clone.forward_ref, bf16[33,256,256]{2,1,0:T(8,128)(2,1)} %constant.9.clone.inverse_ref), custom_call_target="tpu_custom_call" | custom-call | flops 10000000000 | bytes 16000000 | tf_op jit(solution)/shard_map/pallas_call | solution.py:546
  55.1 1.3 copy-done.4
  56.4 3.6 %all-to-all-start.4 = ((bf16[8,256,128]{2,1,0:T(8,128)(2,1)}), bf16[8,256,128]{2,1,0:T(8,128)(2,1)S(1)}, u32[]{:S(2)}, u32[]{:S(2)}) async-start(bf16[8,256,128]{2,1,0:T(8,128)(2,1)} %get-tuple-element.15), calls=%async_computation.4 | async-start | bytes 1048576 | tf_op jit(solution)/shard_map/all_to_all | solution.py:503
  60.1 0.1 copy.22
  60.4 1.4 select_n.19
  61.8 1.3 copy.19.first_ref
  63.0 12.2 %all-to-all-done.4.conv_ref = bf16[8,256,128]{2,1,0:T(8,128)(2,1)S(1)} async-done(((bf16[8,256,128]{2,1,0:T(8,128)(2,1)}), bf16[8,256,128]{2,1,0:T(8,128)(2,1)S(1)}, u32[]{:S(2)}, u32[]{:S(2)}) %all-to-all-start.4) | async-done | bytes 524320 | tf_op jit(solution)/shard_map/all_to_all | solution.py:503
  75.2 1.9 %shard_map.125 = (bf16[4,512,128]{2,1,0:T(8,128)(2,1)}, bf16[512,512]{1,0:T(8,128)(2,1)}, f32[8,32,128]{2,1,0:T(8,128)S(1)}) custom-call(bf16[8,256,128]{2,1,0:T(8,128)(2,1)S(1)} %all-to-all-done.4.conv_ref, bf16[4,512,128]{2,1,0:T(8,128)(2,1)S(1)} %all-to-all-done.back_ref, bf16[512,512]{1,0:T(8,128)(2,1)S(1)} %copy.19.first_ref, bf16[512,512]{1,0:T(8,128)(2,1)S(1)} %copy-done.3), custom_call_target="tpu_custom_call" | custom-call | flops 805306368 | bytes 4194304 | tf_op jit(solution)/shard_map/pallas_call | solution.py:560
  77.1 3.5 %all-to-all-start.5 = ((bf16[4,512,128]{2,1,0:T(8,128)(2,1)}), bf16[4,512,128]{2,1,0:T(8,128)(2,1)S(1)}, u32[]{:S(2)}, u32[]{:S(2)}) async-start(bf16[4,512,128]{2,1,0:T(8,128)(2,1)} %get-tuple-element.17), calls=%async_computation.5 | async-start | bytes 1048576 | tf_op jit(solution)/shard_map/all_to_all | solution.py:503
  80.6 1.4 shard_map.120
  82.0 7.5 %all-to-all-done.5.mix_ref = bf16[4,512,128]{2,1,0:T(8,128)(2,1)S(1)} async-done(((bf16[4,512,128]{2,1,0:T(8,128)(2,1)}), bf16[4,512,128]{2,1,0:T(8,128)(2,1)S(1)}, u32[]{:S(2)}, u32[]{:S(2)}) %all-to-all-start.5) | async-done | bytes 524320 | tf_op jit(solution)/shard_map/all_to_all | solution.py:503
  89.4 3.6 %all-to-all-start.1 = ((bf16[8,256,128]{2,1,0:T(8,128)(2,1)}), bf16[8,256,128]{2,1,0:T(8,128)(2,1)S(1)}, u32[]{:S(2)}, u32[]{:S(2)}) async-start(bf16[8,256,128]{2,1,0:T(8,128)(2,1)} %shard_map.120), calls=%async_computation.1 | async-start | bytes 1048576 | tf_op jit(solution)/shard_map/all_to_all | solution.py:503
  93.0 1.3 shard_map.126
  94.3 13.1 %all-to-all-done.1.grad_ref = bf16[8,256,128]{2,1,0:T(8,128)(2,1)S(1)} async-done(((bf16[8,256,128]{2,1,0:T(8,128)(2,1)}), bf16[8,256,128]{2,1,0:T(8,128)(2,1)S(1)}, u32[]{:S(2)}, u32[]{:S(2)}) %all-to-all-start.1) | async-done | bytes 524320 | tf_op jit(solution)/shard_map/all_to_all | solution.py:503
  107.4 3.6 %all-to-all-start.6 = ((f32[8,48,128]{2,1,0:T(8,128)}), f32[8,48,128]{2,1,0:T(8,128)S(1)}, u32[]{:S(2)}, u32[]{:S(2)}) async-start(f32[8,48,128]{2,1,0:T(8,128)} %shard_map.126), calls=%async_computation.6 | async-start | bytes 393216 | tf_op jit(solution)/shard_map/all_to_all | solution.py:503
  111.0 1.6 %copy-done.5 = bf16[33,256,128]{2,1,0:T(8,128)(2,1)S(1)} copy-done((bf16[33,256,128]{2,1,0:T(8,128)(2,1)S(1)}, bf16[33,256,128]{2,1,0:T(8,128)(2,1)}, u32[]{:S(2)}) %copy-start.5) | copy-done | bytes 2162712
  112.6 14.3 %shard_map.123 = bf16[8,512,128]{2,1,0:T(8,128)(2,1)} custom-call(bf16[8,256,128]{2,1,0:T(8,128)(2,1)S(1)} %all-to-all-done.1.grad_ref, bf16[33,256,128]{2,1,0:T(8,128)(2,1)S(1)} %copy-done.5, bf16[33,256,256]{2,1,0:T(8,128)(2,1)} %constant.8.clone.forward_ref, bf16[33,256,256]{2,1,0:T(8,128)(2,1)} %constant.9.clone.inverse_ref), custom_call_target="tpu_custom_call" | custom-call | flops 10000000000 | bytes 16000000 | tf_op jit(solution)/shard_map/pallas_call | solution.py:556
  127.0 6.0 %all-to-all-start.3 = ((bf16[8,512,128]{2,1,0:T(8,128)(2,1)}), bf16[8,512,128]{2,1,0:T(8,128)(2,1)S(1)}, u32[]{:S(2)}, u32[]{:S(2)}) async-start(bf16[8,512,128]{2,1,0:T(8,128)(2,1)} %shard_map.123), calls=%async_computation.3 | async-start | bytes 2097152 | tf_op jit(solution)/shard_map/all_to_all | solution.py:503
  133.1 0.6 copy.21
  133.7 0.7 reshape.49
  134.4 24.1 %all-to-all-done.3.in_ref = bf16[8,512,128]{2,1,0:T(8,128)(2,1)S(1)} async-done(((bf16[8,512,128]{2,1,0:T(8,128)(2,1)}), bf16[8,512,128]{2,1,0:T(8,128)(2,1)S(1)}, u32[]{:S(2)}, u32[]{:S(2)}) %all-to-all-start.3) | async-done | bytes 1048608 | tf_op jit(solution)/shard_map/all_to_all | solution.py:503
  158.5 1.4 shard_map.124
  (22 shorter events, 0.3 us)
Async XLA Ops:
  0.6 1.0 copy-start.1
  1.7 1.0 copy-start.2
  2.7 8.7 %copy-start.6 = (bf16[16,32,32]{2,1,0:T(8,128)(2,1)S(1)}, bf16[16,32,32]{2,1,0:T(8,128)(2,1)}, u32[]{:S(2)}) copy-start(bf16[16,32,32]{2,1,0:T(8,128)(2,1)} %param.13) | copy-start | bytes 98308
  4.1 33.0 %all-to-all-start.2 = ((bf16[8,512,128]{2,1,0:T(8,128)(2,1)}), bf16[8,512,128]{2,1,0:T(8,128)(2,1)S(1)}, u32[]{:S(2)}, u32[]{:S(2)}) async-start(bf16[8,512,128]{2,1,0:T(8,128)(2,1)} %shard_map.121), calls=%async_computation.2 | async-start | bytes 2097152 | tf_op jit(solution)/shard_map/all_to_all | solution.py:503
  13.0 3.6 %copy-start = (bf16[512,512]{1,0:T(8,128)(2,1)S(1)}, bf16[512,512]{1,0:T(8,128)(2,1)}, u32[]{:S(2)}) copy-start(bf16[512,512]{1,0:T(8,128)(2,1)} %d_out_ref.3) | copy-start | bytes 1572868
  37.1 19.3 %all-to-all-start = ((bf16[4,512,128]{2,1,0:T(8,128)(2,1)}), bf16[4,512,128]{2,1,0:T(8,128)(2,1)S(1)}, u32[]{:S(2)}, u32[]{:S(2)}) async-start(bf16[4,512,128]{2,1,0:T(8,128)(2,1)} %shard_map.119), calls=%async_computation | async-start | bytes 1048576 | tf_op jit(solution)/shard_map/all_to_all | solution.py:503
  40.6 19.4 %copy-start.7 = (bf16[8,64,64]{2,1,0:T(8,128)(2,1)S(1)}, bf16[8,64,64]{2,1,0:T(8,128)(2,1)}, u32[]{:S(2)}) copy-start(bf16[8,64,64]{2,1,0:T(8,128)(2,1)} %param.12) | copy-start | bytes 196612
  55.1 1.3 copy-start.4
  56.4 18.8 %all-to-all-start.4 = ((bf16[8,256,128]{2,1,0:T(8,128)(2,1)}), bf16[8,256,128]{2,1,0:T(8,128)(2,1)S(1)}, u32[]{:S(2)}, u32[]{:S(2)}) async-start(bf16[8,256,128]{2,1,0:T(8,128)(2,1)} %get-tuple-element.15), calls=%async_computation.4 | async-start | bytes 1048576 | tf_op jit(solution)/shard_map/all_to_all | solution.py:503
  60.0 15.2 %copy-start.3 = (bf16[512,512]{1,0:T(8,128)(2,1)S(1)}, bf16[512,512]{1,0:T(8,128)(2,1)}, u32[]{:S(2)}) copy-start(bf16[512,512]{1,0:T(8,128)(2,1)} %gate_ref.3) | copy-start | bytes 1572868
  77.1 12.3 %all-to-all-start.5 = ((bf16[4,512,128]{2,1,0:T(8,128)(2,1)}), bf16[4,512,128]{2,1,0:T(8,128)(2,1)S(1)}, u32[]{:S(2)}, u32[]{:S(2)}) async-start(bf16[4,512,128]{2,1,0:T(8,128)(2,1)} %get-tuple-element.17), calls=%async_computation.5 | async-start | bytes 1048576 | tf_op jit(solution)/shard_map/all_to_all | solution.py:503
  89.4 18.0 %all-to-all-start.1 = ((bf16[8,256,128]{2,1,0:T(8,128)(2,1)}), bf16[8,256,128]{2,1,0:T(8,128)(2,1)S(1)}, u32[]{:S(2)}, u32[]{:S(2)}) async-start(bf16[8,256,128]{2,1,0:T(8,128)(2,1)} %shard_map.120), calls=%async_computation.1 | async-start | bytes 1048576 | tf_op jit(solution)/shard_map/all_to_all | solution.py:503
  107.4 19.6 %all-to-all-start.6 = ((f32[8,48,128]{2,1,0:T(8,128)}), f32[8,48,128]{2,1,0:T(8,128)S(1)}, u32[]{:S(2)}, u32[]{:S(2)}) async-start(f32[8,48,128]{2,1,0:T(8,128)} %shard_map.126), calls=%async_computation.6 | async-start | bytes 393216 | tf_op jit(solution)/shard_map/all_to_all | solution.py:503
  111.0 1.6 %copy-start.5 = (bf16[33,256,128]{2,1,0:T(8,128)(2,1)S(1)}, bf16[33,256,128]{2,1,0:T(8,128)(2,1)}, u32[]{:S(2)}) copy-start(bf16[33,256,128]{2,1,0:T(8,128)(2,1)} %copy-done.4) | copy-start | bytes 6488068
  127.0 31.6 %all-to-all-start.3 = ((bf16[8,512,128]{2,1,0:T(8,128)(2,1)}), bf16[8,512,128]{2,1,0:T(8,128)(2,1)S(1)}, u32[]{:S(2)}, u32[]{:S(2)}) async-start(bf16[8,512,128]{2,1,0:T(8,128)(2,1)} %shard_map.123), calls=%async_computation.3 | async-start | bytes 2097152 | tf_op jit(solution)/shard_map/all_to_all | solution.py:503

commit v2 on v1

--- a/solution.py
+++ b/solution.py
@@ -1,3 +1,4 @@
+import functools
 import math
 
 import jax
@@ -387,12 +388,6 @@
         return carry
 
     lax.fori_loop(0, INNER // CHUNK, last, 0)
-
-
-def back_kernel(d_out_ref, second_ref, out_ref):
-    value = jnp.dot(d_out_ref[...], second_ref[...], preferred_element_type=F32).astype(BF16)
-    for c in range(out_ref.shape[0]):
-        out_ref[c] = value[:, c * LANES : (c + 1) * LANES]
 
 
 def joined(ref):
@@ -489,18 +484,169 @@
             out_ref[c * per + d, first_rows:, :] = piece
 
 
-def call(kernel, outs, scratch=(), flops=0, moved=0):
-    return pl.pallas_call(
-        kernel,
-        out_shape=outs,
-        scratch_shapes=list(scratch),
-        compiler_params=pltpu.CompilerParams(vmem_limit_bytes=48 * 1024 * 1024),
-        cost_estimate=pl.CostEstimate(flops=flops, bytes_accessed=moved, transcendentals=0),
-    )
-
-
-def exchange(value, axis):
-    return lax.all_to_all(value, axis, split_axis=0, concat_axis=0, tiled=True)
+PAIR, BACK, GRAD, CONV, RESULT, MIX, SMALL = range(7)
+
+
+class Exchange:
+    def __init__(self, number, axis, count, send, recv, send_sem, recv_sem):
+        self.axis, self.count, self.send, self.recv = axis, count, send, recv
+        self.number, self.send_sem, self.recv_sem = number, send_sem, recv_sem
+        self.me = lax.axis_index(axis)
+
+    def copy(self, peer, slot):
+        return pltpu.make_async_remote_copy(
+            src_ref=self.send.at[peer],
+            dst_ref=self.recv.at[slot],
+            send_sem=self.send_sem.at[self.number, peer],
+            recv_sem=self.recv_sem.at[self.number, slot],
+            device_id={self.axis: peer},
+            device_id_type=pl.DeviceIdType.MESH,
+        )
+
+    def peers(self):
+        return [lax.rem(self.me + d, self.count) for d in range(1, self.count)]
+
+    def start(self):
+        for peer in self.peers():
+            self.copy(peer, self.me).start()
+        self.recv[self.me] = self.send[self.me]
+
+    def wait_recv(self):
+        for peer in self.peers():
+            self.copy(peer, peer).wait_recv()
+
+    def wait_send(self):
+        for peer in self.peers():
+            self.copy(peer, self.me).wait_send()
+
+
+def spread(values, pick):
+    return jnp.dot(values, pick.astype(F32).astype(BF16), preferred_element_type=F32)
+
+
+def first_matrix(w_ref, blocks, inner):
+    rows, block = w_ref.shape
+    shape = (block, rows)
+    k = lax.broadcasted_iota(jnp.int32, shape, 0)
+    col = lax.broadcasted_iota(jnp.int32, shape, 1)
+    wide = spread(w_ref[...], k == (col // LANES) * inner + col % inner)
+    row = lax.broadcasted_iota(jnp.int32, wide.shape, 0)
+    col = lax.broadcasted_iota(jnp.int32, wide.shape, 1)
+    return jnp.where(row // block == (col % LANES) // inner, wide, 0.0).astype(BF16)
+
+
+def second_matrix(w_ref, inner):
+    rows, width = w_ref.shape
+    across = rows // inner
+    r = lax.broadcasted_iota(jnp.int32, (rows, rows), 0)
+    c = lax.broadcasted_iota(jnp.int32, (rows, rows), 1)
+    order = (c == (r % inner) * across + r // inner).astype(F32).astype(BF16)
+    turned = jnp.dot(order, w_ref[...], preferred_element_type=F32).astype(BF16)
+    o = lax.broadcasted_iota(jnp.int32, (width, inner * width), 0)
+    c = lax.broadcasted_iota(jnp.int32, (width, inner * width), 1)
+    wide = spread(turned, o == c % width)
+    row = lax.broadcasted_iota(jnp.int32, wide.shape, 0)
+    col = lax.broadcasted_iota(jnp.int32, wide.shape, 1)
+    return jnp.where(row % inner == col // width, wide, 0.0).astype(BF16)
+
+
+def whole_kernel(
+    devices,
+    groups,
+    blocks,
+    inner,
+    out_block,
+    signal_ref,
+    filter_ref,
+    gate_ref,
+    d_out_ref,
+    w_first_ref,
+    w_second_ref,
+    forward_hbm,
+    inverse_hbm,
+    grad_signal_ref,
+    grad_filter_ref,
+    grad_gate_ref,
+    small_ref,
+    *scratch,
+):
+    buffers, rest = scratch[:14], scratch[14:]
+    (forward, inverse, spec, y_ref, z_ref, first, grad_first) = rest[:7]
+    table_sem, send_sem, recv_sem = rest[7:]
+    axes = ["seq", "ch", "seq", "seq", "seq", "ch", "seq"]
+    counts = {"seq": devices, "ch": groups}
+    exchanges = [
+        Exchange(n, axis, counts[axis], buffers[2 * n], buffers[2 * n + 1], send_sem, recv_sem)
+        for n, axis in enumerate(axes)
+    ]
+    tables = [
+        pltpu.make_async_copy(forward_hbm, forward, table_sem.at[0]),
+        pltpu.make_async_copy(inverse_hbm, inverse, table_sem.at[1]),
+    ]
+    barrier = pltpu.get_barrier_semaphore()
+    for exchange in (exchanges[PAIR], exchanges[BACK]):
+        for peer in exchange.peers():
+            pl.semaphore_signal(
+                barrier,
+                inc=1,
+                device_id={exchange.axis: peer},
+                device_id_type=pl.DeviceIdType.MESH,
+            )
+    for table in tables:
+        table.start()
+    pack_kernel(signal_ref, filter_ref, exchanges[PAIR].send)
+    pl.semaphore_wait(barrier, devices + groups - 2)
+    exchanges[PAIR].start()
+
+    second = second_matrix(w_second_ref, inner)
+    back = lax.dot_general(
+        d_out_ref[...], second, (((1,), (1,)), ((), ())), preferred_element_type=F32
+    ).astype(BF16)
+    for c in range(groups):
+        exchanges[BACK].send[c] = back[:, c * LANES : (c + 1) * LANES]
+    exchanges[BACK].start()
+    first[...] = first_matrix(w_first_ref, blocks, inner)
+    exchanges[BACK].wait_recv()
+    back_ref = exchanges[BACK].recv
+    grad_conv_kernel(back_ref, first, gate_ref, exchanges[GRAD].send)
+    exchanges[GRAD].start()
+    for table in tables:
+        table.wait()
+    exchanges[PAIR].wait_recv()
+    conv_kernel(
+        exchanges[PAIR].recv, forward, inverse, spec, exchanges[CONV].send, y_ref, z_ref
+    )
+    exchanges[CONV].start()
+    exchanges[GRAD].wait_recv()
+    adjoint_kernel(
+        exchanges[GRAD].recv, spec, forward, inverse, exchanges[RESULT].send, y_ref, z_ref
+    )
+    exchanges[RESULT].start()
+    exchanges[CONV].wait_recv()
+    mix_kernel(
+        exchanges[CONV].recv,
+        back_ref,
+        first,
+        gate_ref,
+        exchanges[MIX].send,
+        grad_gate_ref,
+        grad_first,
+    )
+    exchanges[MIX].start()
+    exchanges[MIX].wait_recv()
+    second_kernel(
+        exchanges[MIX].recv, d_out_ref, grad_first, exchanges[SMALL].send, inner, out_block
+    )
+    exchanges[SMALL].start()
+    exchanges[RESULT].wait_recv()
+    unpack_kernel(exchanges[RESULT].recv, grad_signal_ref, grad_filter_ref)
+    exchanges[SMALL].wait_recv()
+    total = exchanges[SMALL].recv[0]
+    for s in range(1, devices):
+        total = total + exchanges[SMALL].recv[s]
+    small_ref[...] = total
+    for exchange in exchanges:
+        exchange.wait_send()
 
 
 def shards_whole(signal, filter_raw, gate, d_out, w_first, w_second):
@@ -513,87 +659,62 @@
     forward, inverse = (jnp.asarray(t) for t in dft_tables(outer, float(length) ** (-0.5)))
     blocks, block, _ = w_first.shape
     inner, across, out_block = w_second.shape
-    shape = jax.ShapeDtypeStruct
-    scratch = (
-        pltpu.VMEM((classes, 2 * INNER, LANES), BF16),
-        pltpu.VMEM((classes, 2 * INNER, LANES), F32),
-    )
-
-    second_t = w_second.transpose(0, 2, 1).reshape(inner, out_block, groups, blocks, 1)
-    second = jnp.where(
-        jnp.eye(inner, dtype=bool)[:, None, None, None, :], second_t, jnp.zeros((), BF16)
-    ).reshape(width, width)
-    first = jnp.where(
-        jnp.eye(blocks, dtype=bool)[:, None, None, :, None],
-        w_first.reshape(blocks, block, groups, 1, inner),
-        jnp.zeros((), BF16),
-    ).reshape(width, width)
-
-    dense = 2 * rows * width * width
-    back = call(back_kernel, shape((groups, rows, LANES), BF16), flops=dense, moved=1 << 21)(
-        d_out, second
-    )
-    back = exchange(back, "ch")
-    pair = call(pack_kernel, shape((devices, rows, LANES), BF16), flops=1 << 20, moved=1 << 21)(
-        signal, filter_raw
-    )
-    pair = exchange(pair, "seq")
-    grad_conv = call(
-        grad_conv_kernel, shape((devices, rows // 2, LANES), BF16), flops=dense, moved=1 << 21
-    )(back, first, gate)
-    grad_conv = exchange(grad_conv, "seq")
-    cost = dict(flops=10 * 10**9, moved=16 * 10**6)
-    spec, conv = call(
-        conv_kernel,
-        (
-            shape((classes, 2 * INNER, LANES), BF16),
-            shape((devices, rows // 2, LANES), BF16),
+    first_rows = blocks * (block // devices) * block // LANES
+    second_rows = inner * (across // devices) * out_block // LANES
+    small_rows = first_rows + second_rows
+    wide = ((devices, rows, LANES), BF16)
+    half = ((devices, rows // 2, LANES), BF16)
+    mixed = ((groups, rows, LANES), BF16)
+    small = ((devices, small_rows, LANES), F32)
+    buffers = [
+        pltpu.VMEM(*kind)
+        for kind in (wide, mixed, half, half, wide, mixed, small)
+        for _ in range(2)
+    ]
+    vmem = pl.BlockSpec(memory_space=pltpu.VMEM)
+    anywhere = pl.BlockSpec(memory_space=pl.ANY)
+    field = jax.ShapeDtypeStruct((rows, width), BF16)
+    grad_signal, grad_filter, grad_gate, sums = pl.pallas_call(
+        functools.partial(whole_kernel, devices, groups, blocks, inner, out_block),
+        out_shape=(field, field, field, jax.ShapeDtypeStruct((small_rows, LANES), F32)),
+        in_specs=[vmem] * 6 + [anywhere] * 2,
+        out_specs=(vmem,) * 4,
+        scratch_shapes=buffers
+        + [
+            pltpu.VMEM(forward.shape, BF16),
+            pltpu.VMEM(inverse.shape, BF16),
+            pltpu.VMEM((classes, 2 * INNER, LANES), BF16),
+            pltpu.VMEM((classes, 2 * INNER, LANES), BF16),
+            pltpu.VMEM((classes, 2 * INNER, LANES), F32),
+            pltpu.VMEM((width, width), BF16),
+            pltpu.VMEM((devices, first_rows, LANES), F32),
+            pltpu.SemaphoreType.DMA((2,)),
+            pltpu.SemaphoreType.DMA((7, devices)),
+            pltpu.SemaphoreType.DMA((7, devices)),
+        ],
+        compiler_params=pltpu.CompilerParams(
+            collective_id=0, has_side_effects=True, vmem_limit_bytes=50 * 1024 * 1024
         ),
-        scratch,
-        **cost,
-    )(pair, forward, inverse)
-    conv = exchange(conv, "seq")
-    grads = call(adjoint_kernel, shape((devices, rows, LANES), BF16), scratch, **cost)(
-        grad_conv, spec, forward, inverse
-    )
-    first_rows = blocks * (block // devices) * block // LANES
-    mix, grad_gate, grad_first = call(
-        mix_kernel,
-        (
-            shape((groups, rows, LANES), BF16),
-            shape((rows, width), BF16),
-            shape((devices, first_rows, LANES), F32),
+        cost_estimate=pl.CostEstimate(
+            flops=20 * 10**9, bytes_accessed=16 * 10**6, transcendentals=0
         ),
-        flops=3 * dense,
-        moved=1 << 22,
-    )(conv, back, first, gate)
-    mix = exchange(mix, "ch")
-    grads = exchange(grads, "seq")
-
-    def second_body(mix_ref, d_out_ref, grad_first_ref, out_ref):
-        second_kernel(mix_ref, d_out_ref, grad_first_ref, out_ref, inner, out_block)
-
-    second_rows = inner * (across // devices) * out_block // LANES
-    small = call(
-        second_body,
-        shape((devices, first_rows + second_rows, LANES), F32),
-        flops=dense,
-        moved=1 << 21,
-    )(mix, d_out, grad_first)
-    small = exchange(small, "seq").sum(axis=0)
+    )(
+        signal,
+        filter_raw,
+        gate,
+        d_out,
+        w_first.reshape(blocks * block, block),
+        w_second.reshape(inner * across, out_block),
+        forward,
+        inverse,
+    )
     grad_first = (
-        small[:first_rows]
+        sums[:first_rows]
         .reshape(blocks // 2, block // devices, 2, block)
         .transpose(2, 0, 1, 3)
         .reshape(blocks, block // devices, block)
     )
-    grad_second = small[first_rows:].reshape(inner, across // devices, out_block)
-    grad_signal, grad_filter = call(
-        unpack_kernel,
-        (shape((rows, width), BF16), shape((rows, width), BF16)),
-        flops=1 << 20,
-        moved=1 << 21,
-    )(grads)
+    grad_second = sums[first_rows:].reshape(inner, across // devices, out_block)
     return (grad_signal, grad_filter, grad_gate, grad_first, grad_second)
 
 

time: 161 us -> 93.2 us (0.58)
  waiting for transfers between devices: 76.1 us -> 0 us
  Pallas kernels: 37.3 us -> 82.5 us
  starting transfers between devices: 31 us -> 0 us
  local copies, waits for them, and re-layouts: 12.9 us -> 9.75 us
  other arithmetic: 1.72 us -> 0 us
    all_to_all x7 -> x0, waiting for transfers between devices: 76.1 us -> none  [exchange(): return lax.all_to_all(value, axis, split_axis=0, concat_axis=0, tiled=True)]
    pallas_call x8 -> x1, Pallas kernels: 37.3 us -> 82.5 us  [shards_whole(): pl.pallas_call(functools.partial(whole_kernel, devices, groups, blocks, i...]
    all_to_all x7 -> x0, starting transfers between devices: 31 us -> none  [exchange(): return lax.all_to_all(value, axis, split_axis=0, concat_axis=0, tiled=True)]
    select_n x4 -> x0, local copies, waits for them, and re-layouts: 6.29 us -> none  [the longest x2 3.63 us: shards_whole(): jnp.where(jnp.eye(inner, dtype=bool)[:, None, None, None, :], second_t, j...]
    unnamed x16 -> x15, local copies, waits for them, and re-layouts: 5.05 us -> 8.34 us
    select_n x2 -> x0, other arithmetic: 1.69 us -> none  [the longest x1 1.55 us: shards_whole(): jnp.where(jnp.eye(inner, dtype=bool)[:, None, None, None, :], second_t, j...]
  transfers between devices with their start and end apart: 7 -> 0, of which waited for: 5 -> 0; matrix products, arithmetic and copies ran while one was open for 6% -> 0% of each run, Pallas kernels for 20% -> 0%
where the time goes in v2:
time: 93.2 us; the launch traced here: 92.9 us
  Pallas kernels  82.5 us (89%)
  local copies, waits for them, and re-layouts  9.75 us (10%)
    pallas_call x1, Pallas kernels, shards_whole(): pl.pallas_call(functools.partial(whole_kernel, devices, groups, blocks, i...  82.5 us
    unnamed x15, local copies, waits for them, and re-layouts  8.34 us

profile of v2, /device:TPU:0, one launch (start us, length us, event | category | flops | bytes accessed | tf_op | source)
XLA Modules:
  0.0 92.9 jit_solution(10881921191664277373)
XLA Ops:
  0.6 0.0 copy-start
  0.6 1.0 %copy-done = bf16[512,512]{1,0:T(8,128)(2,1)S(1)} copy-done((bf16[512,512]{1,0:T(8,128)(2,1)S(1)}, bf16[512,512]{1,0:T(8,128)(2,1)}, u32[]{:S(2)}) %copy-start) | copy-done | bytes 524312
  1.7 0.0 copy-start.1
  1.7 1.0 %copy-done.1 = bf16[512,512]{1,0:T(8,128)(2,1)S(1)} copy-done((bf16[512,512]{1,0:T(8,128)(2,1)S(1)}, bf16[512,512]{1,0:T(8,128)(2,1)}, u32[]{:S(2)}) %copy-start.1) | copy-done | bytes 524312
  2.7 0.0 copy-start.2
  2.7 1.0 %copy-done.2 = bf16[512,512]{1,0:T(8,128)(2,1)S(1)} copy-done((bf16[512,512]{1,0:T(8,128)(2,1)S(1)}, bf16[512,512]{1,0:T(8,128)(2,1)}, u32[]{:S(2)}) %copy-start.2) | copy-done | bytes 524312
  3.8 0.0 copy-start.3
  3.8 1.0 %copy-done.3 = bf16[512,512]{1,0:T(8,128)(2,1)S(1)} copy-done((bf16[512,512]{1,0:T(8,128)(2,1)S(1)}, bf16[512,512]{1,0:T(8,128)(2,1)}, u32[]{:S(2)}) %copy-start.3) | copy-done | bytes 524312
  4.8 0.0 copy-start.4
  4.8 0.9 copy-done.4
  5.7 0.0 copy-start.5
  5.7 0.9 copy-done.5
  6.6 82.5 %shard_map.119 = (bf16[512,512]{1,0:T(8,128)(2,1)S(1)}, bf16[512,512]{1,0:T(8,128)(2,1)S(1)}, bf16[512,512]{1,0:T(8,128)(2,1)S(1)}, f32[48,128]{1,0:T(8,128)S(1)}) custom-call(bf16[512,512]{1,0:T(8,128)(2,1)S(1)} %copy-done, bf16[512,512]{1,0:T(8,128)(2,1)S(1)} %copy-done.1, bf16[512,512]{1,0:T(8,128)(2,1)S(1)} %copy-done.2, bf16[512,512]{1,0:T(8,128)(2,1)S(1)} %copy-done.3, ...), custom_call_target="tpu_custom_call" | custom-call | flops 20000000000 | bytes 16000000 | tf_op jit(solution)/shard_map/pallas_call | solution.py:677
  89.1 0.1 reshape.27
  89.2 0.6 copy.13
  89.8 0.7 reshape.29
  90.5 0.8 copy.17
  91.3 0.8 copy.18
  92.1 0.8 copy.19
  (2 shorter events, 0.0 us)
Async XLA Ops:
  0.6 1.0 %copy-start = (bf16[512,512]{1,0:T(8,128)(2,1)S(1)}, bf16[512,512]{1,0:T(8,128)(2,1)}, u32[]{:S(2)}) copy-start(bf16[512,512]{1,0:T(8,128)(2,1)} %signal_ref.1) | copy-start | bytes 1572868
  1.7 1.0 %copy-start.1 = (bf16[512,512]{1,0:T(8,128)(2,1)S(1)}, bf16[512,512]{1,0:T(8,128)(2,1)}, u32[]{:S(2)}) copy-start(bf16[512,512]{1,0:T(8,128)(2,1)} %filter_ref.1) | copy-start | bytes 1572868
  2.7 1.0 %copy-start.2 = (bf16[512,512]{1,0:T(8,128)(2,1)S(1)}, bf16[512,512]{1,0:T(8,128)(2,1)}, u32[]{:S(2)}) copy-start(bf16[512,512]{1,0:T(8,128)(2,1)} %gate_ref.1) | copy-start | bytes 1572868
  3.8 1.0 %copy-start.3 = (bf16[512,512]{1,0:T(8,128)(2,1)S(1)}, bf16[512,512]{1,0:T(8,128)(2,1)}, u32[]{:S(2)}) copy-start(bf16[512,512]{1,0:T(8,128)(2,1)} %d_out_ref.1) | copy-start | bytes 1572868
  4.8 0.9 copy-start.4
  5.7 0.9 copy-start.5

commit v3 on v2

--- a/solution.py
+++ b/solution.py
@@ -189,6 +189,7 @@
 HALF = 64
 INNER = 128
 CHUNK = 16
+PARTS = 2
 
 
 def dft_tables(outer, scale):
@@ -283,44 +284,55 @@
     return out
 
 
-def pack_kernel(signal_ref, filter_ref, out_ref):
-    rows = signal_ref.shape[0]
-    low = low_lanes(rows)
+def pack_part(signal_ref, filter_ref, out_ref, part):
+    size = INNER // PARTS
+    low = low_lanes(size)
     for p in range(out_ref.shape[0] // 2):
         cols = slice(p * LANES, (p + 1) * LANES)
-        a = signal_ref[:, cols].astype(F32)
-        b = filter_ref[:, cols].astype(F32)
-        out_ref[2 * p] = jnp.where(low, a, swap(b)).astype(BF16)
-        out_ref[2 * p + 1] = jnp.where(low, swap(a), b).astype(BF16)
-
-
-def unpack_kernel(in_ref, signal_ref, filter_ref):
-    rows = signal_ref.shape[0]
-    low = low_lanes(rows)
+        for m in range(signal_ref.shape[0] // INNER):
+            source = slice(m * INNER + part * size, m * INNER + (part + 1) * size)
+            rows = slice(m * size, (m + 1) * size)
+            a = signal_ref[source, cols].astype(F32)
+            b = filter_ref[source, cols].astype(F32)
+            out_ref[2 * p, rows, :] = jnp.where(low, a, swap(b)).astype(BF16)
+            out_ref[2 * p + 1, rows, :] = jnp.where(low, swap(a), b).astype(BF16)
+
+
+def unpack_part(in_ref, signal_ref, filter_ref, part):
+    size = INNER // PARTS
+    low = low_lanes(size)
     for p in range(in_ref.shape[0] // 2):
         cols = slice(p * LANES, (p + 1) * LANES)
-        a = in_ref[2 * p].astype(F32)
-        b = in_ref[2 * p + 1].astype(F32)
-        filter_ref[:, cols] = jnp.where(low, a, swap(b)).astype(BF16)
-        signal_ref[:, cols] = jnp.where(low, swap(a), b).astype(BF16)
-
-
-def conv_kernel(pair_ref, forward_ref, inverse_ref, spec_ref, conv_ref, y_ref, z_ref):
-    devices, rows, _ = pair_ref.shape
-    classes = forward_ref.shape[0]
-    outer = 2 * (classes - 1)
-    tiles = rows // INNER
+        for m in range(signal_ref.shape[0] // INNER):
+            target = slice(m * INNER + part * size, m * INNER + (part + 1) * size)
+            rows = slice(m * size, (m + 1) * size)
+            a = in_ref[2 * p, rows, :].astype(F32)
+            b = in_ref[2 * p + 1, rows, :].astype(F32)
+            filter_ref[target, cols] = jnp.where(low, a, swap(b)).astype(BF16)
+            signal_ref[target, cols] = jnp.where(low, swap(a), b).astype(BF16)
+
+
+def conv_first(pair_ref, y_ref, part, outer):
+    size = INNER // PARTS
+    tiles = outer // 2 // pair_ref.shape[0]
 
     def first(j, carry):
         at = pl.multiple_of(j * CHUNK, CHUNK)
         points = [
-            pair_ref[a // tiles, pl.ds((a % tiles) * INNER + at, CHUNK), :].astype(F32)
+            pair_ref[a // tiles, pl.ds((a % tiles) * size + at, CHUNK), :].astype(F32)
             for a in range(outer // 2)
         ]
-        store_classes(y_ref, at, real_dft(points, outer))
+        store_classes(y_ref, part * size + at, real_dft(points, outer))
         return carry
 
-    lax.fori_loop(0, INNER // CHUNK, first, 0)
+    lax.fori_loop(0, size // CHUNK, first, 0)
+
+
+def conv_kernel(forward_ref, inverse_ref, spec_ref, conv_ref, y_ref, z_ref):
+    devices, packed, _ = conv_ref.shape
+    classes = forward_ref.shape[0]
+    outer = 2 * (classes - 1)
+    tiles = 2 * packed // INNER
 
     def middle(q, carry):
         x = jnp.dot(forward_ref[q], y_ref[q], preferred_element_type=F32)
@@ -348,7 +360,7 @@
     lax.fori_loop(0, INNER // CHUNK, last, 0)
 
 
-def adjoint_kernel(grad_ref, spec_ref, forward_ref, inverse_ref, out_ref, y_ref, z_ref):
+def adjoint_kernel(grad_ref, spec_ref, forward_ref, inverse_ref, y_ref, z_ref):
     devices, packed, _ = grad_ref.shape
     classes = forward_ref.shape[0]
     outer = 2 * (classes - 1)
@@ -380,14 +392,22 @@
 
     lax.fori_loop(0, classes, middle, 0, unroll=3)
 
+
+def adjoint_last(z_ref, out_ref, part):
+    size = INNER // PARTS
+    classes = z_ref.shape[0]
+    outer = 2 * (classes - 1)
+    tiles = outer // 2 // out_ref.shape[0]
+
     def last(j, carry):
         at = pl.multiple_of(j * CHUNK, CHUNK)
-        points = real_inverse(load_classes(z_ref, at, classes), outer)
+        points = real_inverse(load_classes(z_ref, part * size + at, classes), outer)
         for a in range(outer // 2):
-            out_ref[a // tiles, pl.ds((a % tiles) * INNER + at, CHUNK), :] = points[a].astype(BF16)
+            rows = pl.ds((a % tiles) * size + at, CHUNK)
+            out_ref[a // tiles, rows, :] = points[a].astype(BF16)
         return carry
 
-    lax.fori_loop(0, INNER // CHUNK, last, 0)
+    lax.fori_loop(0, size // CHUNK, last, 0)
 
 
 def joined(ref):
@@ -485,6 +505,7 @@
 
 
 PAIR, BACK, GRAD, CONV, RESULT, MIX, SMALL = range(7)
+INPUTS = 6
 
 
 class Exchange:
@@ -556,35 +577,36 @@
     blocks,
     inner,
     out_block,
-    signal_ref,
-    filter_ref,
-    gate_ref,
-    d_out_ref,
-    w_first_ref,
-    w_second_ref,
-    forward_hbm,
-    inverse_hbm,
-    grad_signal_ref,
-    grad_filter_ref,
-    grad_gate_ref,
-    small_ref,
-    *scratch,
+    *refs,
 ):
-    buffers, rest = scratch[:14], scratch[14:]
+    inputs, (forward_hbm, inverse_hbm) = refs[:INPUTS], refs[INPUTS : INPUTS + 2]
+    refs = refs[INPUTS + 2 :]
+    grad_signal_ref, grad_filter_ref, grad_gate_ref, small_ref = refs[:4]
+    buffers, local, rest = refs[4:18], refs[18 : 18 + INPUTS], refs[18 + INPUTS :]
     (forward, inverse, spec, y_ref, z_ref, first, grad_first) = rest[:7]
-    table_sem, send_sem, recv_sem = rest[7:]
+    input_sem, send_sem, recv_sem = rest[7:]
+    signal_ref, filter_ref, gate_ref, d_out_ref, w_first_ref, w_second_ref = local
     axes = ["seq", "ch", "seq", "seq", "seq", "ch", "seq"]
     counts = {"seq": devices, "ch": groups}
-    exchanges = [
-        Exchange(n, axis, counts[axis], buffers[2 * n], buffers[2 * n + 1], send_sem, recv_sem)
-        for n, axis in enumerate(axes)
-    ]
-    tables = [
-        pltpu.make_async_copy(forward_hbm, forward, table_sem.at[0]),
-        pltpu.make_async_copy(inverse_hbm, inverse, table_sem.at[1]),
+    exchanges = {}
+    number = 0
+    for n, axis in enumerate(axes):
+        send, recv = buffers[2 * n], buffers[2 * n + 1]
+        cut = n in (PAIR, RESULT)
+        made = []
+        for part in range(PARTS if cut else 1):
+            ends = (send.at[part], recv.at[part]) if cut else (send, recv)
+            made.append(Exchange(number, axis, counts[axis], *ends, send_sem, recv_sem))
+            number += 1
+        exchanges[n] = made if cut else made[0]
+    copies = [
+        pltpu.make_async_copy(source, target, input_sem.at[n])
+        for n, (source, target) in enumerate(
+            zip((*inputs, forward_hbm, inverse_hbm), (*local, forward, inverse))
+        )
     ]
     barrier = pltpu.get_barrier_semaphore()
-    for exchange in (exchanges[PAIR], exchanges[BACK]):
+    for exchange in (exchanges[GRAD], exchanges[BACK]):
         for peer in exchange.peers():
             pl.semaphore_signal(
                 barrier,
@@ -592,11 +614,18 @@
                 device_id={exchange.axis: peer},
                 device_id_type=pl.DeviceIdType.MESH,
             )
-    for table in tables:
-        table.start()
-    pack_kernel(signal_ref, filter_ref, exchanges[PAIR].send)
+    for copy in copies:
+        copy.start()
+    copies[0].wait()
+    copies[1].wait()
+    pack_part(signal_ref, filter_ref, exchanges[PAIR][0].send, 0)
     pl.semaphore_wait(barrier, devices + groups - 2)
-    exchanges[PAIR].start()
+    exchanges[PAIR][0].start()
+    for part in range(1, PARTS):
+        pack_part(signal_ref, filter_ref, exchanges[PAIR][part].send, part)
+        exchanges[PAIR][part].start()
+    for copy in copies[2:INPUTS]:
+        copy.wait()
 
     second = second_matrix(w_second_ref, inner)
     back = lax.dot_general(
@@ -609,19 +638,24 @@
     exchanges[BACK].wait_recv()
     back_ref = exchanges[BACK].recv
     grad_conv_kernel(back_ref, first, gate_ref, exchanges[GRAD].send)
+    outer = 2 * (forward.shape[0] - 1)
+    exchanges[PAIR][0].wait_recv()
+    conv_first(exchanges[PAIR][0].recv, y_ref, 0, outer)
+    for part in range(PARTS):
+        exchanges[PAIR][part].wait_send()
     exchanges[GRAD].start()
-    for table in tables:
-        table.wait()
-    exchanges[PAIR].wait_recv()
-    conv_kernel(
-        exchanges[PAIR].recv, forward, inverse, spec, exchanges[CONV].send, y_ref, z_ref
-    )
+    for part in range(1, PARTS):
+        exchanges[PAIR][part].wait_recv()
+        conv_first(exchanges[PAIR][part].recv, y_ref, part, outer)
+    for copy in copies[INPUTS:]:
+        copy.wait()
+    conv_kernel(forward, inverse, spec, exchanges[CONV].send, y_ref, z_ref)
     exchanges[CONV].start()
     exchanges[GRAD].wait_recv()
-    adjoint_kernel(
-        exchanges[GRAD].recv, spec, forward, inverse, exchanges[RESULT].send, y_ref, z_ref
-    )
-    exchanges[RESULT].start()
+    adjoint_kernel(exchanges[GRAD].recv, spec, forward, inverse, y_ref, z_ref)
+    for part in range(PARTS):
+        adjoint_last(z_ref, exchanges[RESULT][part].send, part)
+        exchanges[RESULT][part].start()
     exchanges[CONV].wait_recv()
     mix_kernel(
         exchanges[CONV].recv,
@@ -638,14 +672,17 @@
         exchanges[MIX].recv, d_out_ref, grad_first, exchanges[SMALL].send, inner, out_block
     )
     exchanges[SMALL].start()
-    exchanges[RESULT].wait_recv()
-    unpack_kernel(exchanges[RESULT].recv, grad_signal_ref, grad_filter_ref)
+    for part in range(PARTS):
+        exchanges[RESULT][part].wait_recv()
+        unpack_part(exchanges[RESULT][part].recv, grad_signal_ref, grad_filter_ref, part)
     exchanges[SMALL].wait_recv()
     total = exchanges[SMALL].recv[0]
     for s in range(1, devices):
         total = total + exchanges[SMALL].recv[s]
     small_ref[...] = total
-    for exchange in exchanges:
+    for n in (BACK, GRAD, CONV, MIX, SMALL):
+        exchanges[n].wait_send()
+    for exchange in exchanges[RESULT]:
         exchange.wait_send()
 
 
@@ -662,7 +699,7 @@
     first_rows = blocks * (block // devices) * block // LANES
     second_rows = inner * (across // devices) * out_block // LANES
     small_rows = first_rows + second_rows
-    wide = ((devices, rows, LANES), BF16)
+    wide = ((PARTS, devices, rows // PARTS, LANES), BF16)
     half = ((devices, rows // 2, LANES), BF16)
     mixed = ((groups, rows, LANES), BF16)
     small = ((devices, small_rows, LANES), F32)
@@ -677,10 +714,13 @@
     grad_signal, grad_filter, grad_gate, sums = pl.pallas_call(
         functools.partial(whole_kernel, devices, groups, blocks, inner, out_block),
         out_shape=(field, field, field, jax.ShapeDtypeStruct((small_rows, LANES), F32)),
-        in_specs=[vmem] * 6 + [anywhere] * 2,
+        in_specs=[anywhere] * (INPUTS + 2),
         out_specs=(vmem,) * 4,
         scratch_shapes=buffers
+        + [pltpu.VMEM((rows, width), BF16)] * 4
         + [
+            pltpu.VMEM((blocks * block, block), BF16),
+            pltpu.VMEM((inner * across, out_block), BF16),
             pltpu.VMEM(forward.shape, BF16),
             pltpu.VMEM(inverse.shape, BF16),
             pltpu.VMEM((classes, 2 * INNER, LANES), BF16),
@@ -688,12 +728,12 @@
             pltpu.VMEM((classes, 2 * INNER, LANES), F32),
             pltpu.VMEM((width, width), BF16),
             pltpu.VMEM((devices, first_rows, LANES), F32),
-            pltpu.SemaphoreType.DMA((2,)),
-            pltpu.SemaphoreType.DMA((7, devices)),
-            pltpu.SemaphoreType.DMA((7, devices)),
+            pltpu.SemaphoreType.DMA((INPUTS + 2,)),
+            pltpu.SemaphoreType.DMA((5 + 2 * PARTS, devices)),
+            pltpu.SemaphoreType.DMA((5 + 2 * PARTS, devices)),
         ],
         compiler_params=pltpu.CompilerParams(
-            collective_id=0, has_side_effects=True, vmem_limit_bytes=50 * 1024 * 1024
+            collective_id=0, has_side_effects=True, vmem_limit_bytes=60 * 1024 * 1024
         ),
         cost_estimate=pl.CostEstimate(
             flops=20 * 10**9, bytes_accessed=16 * 10**6, transcendentals=0

time: 93.2 us -> 94.2 us (1.011)
  Pallas kernels: 82.5 us -> 84.8 us
  local copies, waits for them, and re-layouts: 9.75 us -> 8.43 us
    unnamed x15 -> x3, local copies, waits for them, and re-layouts: 8.34 us -> 5.6 us
    pallas_call x1, Pallas kernels: 82.5 us -> 84.8 us  [shards_whole(): pl.pallas_call(functools.partial(whole_kernel, devices, groups, blocks, i...]
where the time goes in v3:
time: 94.2 us; the launch traced here: 93.9 us
  Pallas kernels  84.8 us (90%)
  local copies, waits for them, and re-layouts  8.43 us (9%)
    pallas_call x1, Pallas kernels, shards_whole(): pl.pallas_call(functools.partial(whole_kernel, devices, groups, blocks, i...  84.8 us
    unnamed x3, local copies, waits for them, and re-layouts  5.6 us

profile of v3, /device:TPU:0, one launch (start us, length us, event | category | flops | bytes accessed | tf_op | source)
XLA Modules:
  0.0 93.9 jit_solution(7938257181645404622)
XLA Ops:
  0.6 84.8 %shard_map.119 = (bf16[512,512]{1,0:T(8,128)(2,1)}, bf16[512,512]{1,0:T(8,128)(2,1)}, bf16[512,512]{1,0:T(8,128)(2,1)}, f32[48,128]{1,0:T(8,128)}) custom-call(bf16[512,512]{1,0:T(8,128)(2,1)} %refs_0_.1, bf16[512,512]{1,0:T(8,128)(2,1)} %refs_1_.1, bf16[512,512]{1,0:T(8,128)(2,1)} %refs_2_.1, bf16[512,512]{1,0:T(8,128)(2,1)} %refs_3_.1, ...), custom_call_target="tpu_custom_call" | custom-call | flops 20000000000 | bytes 16000000 | tf_op jit(solution)/shard_map/pallas_call | solution.py:714
  85.4 0.7 slice.6
  86.1 0.1 reshape.27
  86.2 0.6 copy.13
  86.9 0.7 slice.7
  87.6 0.7 reshape.29
  88.3 1.9 %copy.17 = bf16[512,512]{1,0:T(8,128)(2,1)} copy(bf16[512,512]{1,0:T(8,128)(2,1)} %get-tuple-element.18) | data formatting | bytes 1048576
  90.1 1.9 %copy.18 = bf16[512,512]{1,0:T(8,128)(2,1)} copy(bf16[512,512]{1,0:T(8,128)(2,1)} %get-tuple-element.19) | data formatting | bytes 1048576
  92.0 1.9 %copy.19 = bf16[512,512]{1,0:T(8,128)(2,1)} copy(bf16[512,512]{1,0:T(8,128)(2,1)} %get-tuple-element.20) | data formatting | bytes 1048576

commit v4 on v3

--- a/solution.py
+++ b/solution.py
@@ -343,7 +343,7 @@
         z_ref[q] = jnp.dot(inverse_ref[q], mixed.astype(BF16), preferred_element_type=F32)
         return carry
 
-    lax.fori_loop(0, classes, middle, 0, unroll=3)
+    lax.fori_loop(0, classes, middle, 0, unroll=11)
     low = low_lanes(CHUNK)
     halves = tiles // 2
 
@@ -390,7 +390,7 @@
         z_ref[q] = jnp.dot(inverse_ref[q], mixed.astype(BF16), preferred_element_type=F32)
         return carry
 
-    lax.fori_loop(0, classes, middle, 0, unroll=3)
+    lax.fori_loop(0, classes, middle, 0, unroll=11)
 
 
 def adjoint_last(z_ref, out_ref, part):
@@ -525,7 +525,10 @@
         )
 
     def peers(self):
-        return [lax.rem(self.me + d, self.count) for d in range(1, self.count)]
+        half = self.count // 2
+        own = half * (self.me // half)
+        far = [half - own + lax.rem(self.me + d, half) for d in range(half)]
+        return far + [own + lax.rem(self.me + d, half) for d in range(1, half)]
 
     def start(self):
         for peer in self.peers():
@@ -684,6 +687,26 @@
         exchanges[n].wait_send()
     for exchange in exchanges[RESULT]:
         exchange.wait_send()
+
+
+def finish_kernel(
+    signal_ref, filter_ref, gate_ref, small_ref, signal_out, filter_out, gate_out, first_out, second_out
+):
+    signal_out[...] = signal_ref[...]
+    filter_out[...] = filter_ref[...]
+    gate_out[...] = gate_ref[...]
+    blocks, piece, block = first_out.shape
+    pairs = blocks // 2
+    for i in range(pairs):
+        value = small_ref[i * piece : (i + 1) * piece, :]
+        first_out[i] = value[:, :block]
+        first_out[i + pairs] = swap(value)[:, :block]
+    inner, across, width = second_out.shape
+    value = small_ref[pairs * piece :, :]
+    for i in range(across):
+        part = value if i == 0 else pltpu.roll(value, LANES - i * width, 1)
+        for k in range(inner):
+            second_out[k, i : i + 1, :] = part[k : k + 1, :width]
 
 
 def shards_whole(signal, filter_raw, gate, d_out, w_first, w_second):
@@ -748,14 +771,18 @@
         forward,
         inverse,
     )
-    grad_first = (
-        sums[:first_rows]
-        .reshape(blocks // 2, block // devices, 2, block)
-        .transpose(2, 0, 1, 3)
-        .reshape(blocks, block // devices, block)
-    )
-    grad_second = sums[first_rows:].reshape(inner, across // devices, out_block)
-    return (grad_signal, grad_filter, grad_gate, grad_first, grad_second)
+    shape = jax.ShapeDtypeStruct
+    return pl.pallas_call(
+        finish_kernel,
+        out_shape=(
+            field,
+            field,
+            field,
+            shape((blocks, block // devices, block), F32),
+            shape((inner, across // devices, out_block), F32),
+        ),
+        compiler_params=pltpu.CompilerParams(vmem_limit_bytes=60 * 1024 * 1024),
+    )(grad_signal, grad_filter, grad_gate, sums)
 
 
 def shards(signal, filter_raw, gate, d_out, w_first, w_second):

time: 94.2 us -> 85.5 us (0.908)
  local copies, waits for them, and re-layouts: 8.43 us -> 0 us
    unnamed x3 -> x0, local copies, waits for them, and re-layouts: 5.6 us -> none
    pallas_call x1, Pallas kernels: 84.8 us -> 82.1 us  [shards_whole(): pl.pallas_call(functools.partial(whole_kernel, devices, groups, blocks, i...]
    pallas_call x0 -> x1, Pallas kernels: none -> 2.55 us  [shards_whole(): pl.pallas_call(finish_kernel, out_shape=(field, field, field, shape((bloc...]
    slice x2 -> x0, local copies, waits for them, and re-layouts: 1.42 us -> none  [the longest x1 0.72 us: shards_whole(): sums[:first_rows].reshape(blocks // 2, block // devices, 2, block)]
where the time goes in v4:
time: 85.5 us; the launch traced here: 85.3 us
  Pallas kernels  84.7 us (99%)
    pallas_call x1, Pallas kernels, shards_whole(): pl.pallas_call(functools.partial(whole_kernel, devices, groups, blocks, i...  82.1 us
    pallas_call x1, Pallas kernels, shards_whole(): pl.pallas_call(finish_kernel, out_shape=(field, field, field, shape((bloc...  2.55 us

profile of v4, /device:TPU:0, one launch (start us, length us, event | category | flops | bytes accessed | tf_op | source)
XLA Modules:
  0.0 85.3 jit_solution(1181894092480138513)
XLA Ops:
  0.6 82.1 %shard_map.119 = (bf16[512,512]{1,0:T(8,128)(2,1)}, bf16[512,512]{1,0:T(8,128)(2,1)}, bf16[512,512]{1,0:T(8,128)(2,1)}, f32[48,128]{1,0:T(8,128)}) custom-call(bf16[512,512]{1,0:T(8,128)(2,1)} %refs_0_.1, bf16[512,512]{1,0:T(8,128)(2,1)} %refs_1_.1, bf16[512,512]{1,0:T(8,128)(2,1)} %refs_2_.1, bf16[512,512]{1,0:T(8,128)(2,1)} %refs_3_.1, ...), custom_call_target="tpu_custom_call" | custom-call | flops 20000000000 | bytes 16000000 | tf_op jit(solution)/shard_map/pallas_call | solution.py:737
  82.8 2.6 %shard_map.120 = (bf16[512,512]{1,0:T(8,128)(2,1)}, bf16[512,512]{1,0:T(8,128)(2,1)}, bf16[512,512]{1,0:T(8,128)(2,1)}, f32[8,8,64]{2,1,0:T(8,128)}, f32[16,4,32]{2,1,0:T(4,128)}) custom-call(bf16[512,512]{1,0:T(8,128)(2,1)} %get-tuple-element.9.signal_ref, bf16[512,512]{1,0:T(8,128)(2,1)} %get-tuple-element.10.filter_ref, ...), custom_call_target="tpu_custom_call" | custom-call | tf_op jit(solution)/shard_map/pallas_call | solution.py:775

commit v5 on v4

--- a/solution.py
+++ b/solution.py
@@ -617,13 +617,15 @@
                 device_id={exchange.axis: peer},
                 device_id_type=pl.DeviceIdType.MESH,
             )
-    for copy in copies:
+    for copy in copies[:2]:
         copy.start()
-    copies[0].wait()
-    copies[1].wait()
+    for copy in copies[:2]:
+        copy.wait()
     pack_part(signal_ref, filter_ref, exchanges[PAIR][0].send, 0)
     pl.semaphore_wait(barrier, devices + groups - 2)
     exchanges[PAIR][0].start()
+    for copy in copies[2:]:
+        copy.start()
     for part in range(1, PARTS):
         pack_part(signal_ref, filter_ref, exchanges[PAIR][part].send, part)
         exchanges[PAIR][part].start()

time: 85.5 us -> 85.5 us (level)
  no operation moved by 1% of the time
where the time goes in v5:
time: 85.5 us; the launch traced here: 85.4 us
  Pallas kernels  84.7 us (99%)
    pallas_call x1, Pallas kernels, shards_whole(): pl.pallas_call(functools.partial(whole_kernel, devices, groups, blocks, i...  82.2 us
    pallas_call x1, Pallas kernels, shards_whole(): pl.pallas_call(finish_kernel, out_shape=(field, field, field, shape((bloc...  2.55 us

profile of v5, /device:TPU:0, one launch (start us, length us, event | category | flops | bytes accessed | tf_op | source)
XLA Modules:
  0.0 85.4 jit_solution(10626080468251911640)
XLA Ops:
  0.6 82.2 %shard_map.119 = (bf16[512,512]{1,0:T(8,128)(2,1)}, bf16[512,512]{1,0:T(8,128)(2,1)}, bf16[512,512]{1,0:T(8,128)(2,1)}, f32[48,128]{1,0:T(8,128)}) custom-call(bf16[512,512]{1,0:T(8,128)(2,1)} %refs_0_.1, bf16[512,512]{1,0:T(8,128)(2,1)} %refs_1_.1, bf16[512,512]{1,0:T(8,128)(2,1)} %refs_2_.1, bf16[512,512]{1,0:T(8,128)(2,1)} %refs_3_.1, ...), custom_call_target="tpu_custom_call" | custom-call | flops 20000000000 | bytes 16000000 | tf_op jit(solution)/shard_map/pallas_call | solution.py:739
  82.8 2.6 %shard_map.120 = (bf16[512,512]{1,0:T(8,128)(2,1)}, bf16[512,512]{1,0:T(8,128)(2,1)}, bf16[512,512]{1,0:T(8,128)(2,1)}, f32[8,8,64]{2,1,0:T(8,128)}, f32[16,4,32]{2,1,0:T(4,128)}) custom-call(bf16[512,512]{1,0:T(8,128)(2,1)} %get-tuple-element.9.signal_ref, bf16[512,512]{1,0:T(8,128)(2,1)} %get-tuple-element.10.filter_ref, ...), custom_call_target="tpu_custom_call" | custom-call | tf_op jit(solution)/shard_map/pallas_call | solution.py:777

commit v6 on v5

--- a/solution.py
+++ b/solution.py
@@ -646,8 +646,7 @@
     outer = 2 * (forward.shape[0] - 1)
     exchanges[PAIR][0].wait_recv()
     conv_first(exchanges[PAIR][0].recv, y_ref, 0, outer)
-    for part in range(PARTS):
-        exchanges[PAIR][part].wait_send()
+    exchanges[PAIR][0].wait_send()
     exchanges[GRAD].start()
     for part in range(1, PARTS):
         exchanges[PAIR][part].wait_recv()
@@ -687,7 +686,7 @@
     small_ref[...] = total
     for n in (BACK, GRAD, CONV, MIX, SMALL):
         exchanges[n].wait_send()
-    for exchange in exchanges[RESULT]:
+    for exchange in exchanges[PAIR][1:] + exchanges[RESULT]:
         exchange.wait_send()
 
 

time: 85.5 us -> 85.5 us (level)
  no operation moved by 1% of the time
where the time goes in v6:
time: 85.5 us; the launch traced here: 85.3 us
  Pallas kernels  84.6 us (99%)
    pallas_call x1, Pallas kernels, shards_whole(): pl.pallas_call(functools.partial(whole_kernel, devices, groups, blocks, i...  82.1 us
    pallas_call x1, Pallas kernels, shards_whole(): pl.pallas_call(finish_kernel, out_shape=(field, field, field, shape((bloc...  2.55 us

profile of v6, /device:TPU:0, one launch (start us, length us, event | category | flops | bytes accessed | tf_op | source)
XLA Modules:
  0.0 85.3 jit_solution(15507825492247256058)
XLA Ops:
  0.6 82.1 %shard_map.119 = (bf16[512,512]{1,0:T(8,128)(2,1)}, bf16[512,512]{1,0:T(8,128)(2,1)}, bf16[512,512]{1,0:T(8,128)(2,1)}, f32[48,128]{1,0:T(8,128)}) custom-call(bf16[512,512]{1,0:T(8,128)(2,1)} %refs_0_.1, bf16[512,512]{1,0:T(8,128)(2,1)} %refs_1_.1, bf16[512,512]{1,0:T(8,128)(2,1)} %refs_2_.1, bf16[512,512]{1,0:T(8,128)(2,1)} %refs_3_.1, ...), custom_call_target="tpu_custom_call" | custom-call | flops 20000000000 | bytes 16000000 | tf_op jit(solution)/shard_map/pallas_call | solution.py:738
  82.7 2.6 %shard_map.120 = (bf16[512,512]{1,0:T(8,128)(2,1)}, bf16[512,512]{1,0:T(8,128)(2,1)}, bf16[512,512]{1,0:T(8,128)(2,1)}, f32[8,8,64]{2,1,0:T(8,128)}, f32[16,4,32]{2,1,0:T(4,128)}) custom-call(bf16[512,512]{1,0:T(8,128)(2,1)} %get-tuple-element.9.signal_ref, bf16[512,512]{1,0:T(8,128)(2,1)} %get-tuple-element.10.filter_ref, ...), custom_call_target="tpu_custom_call" | custom-call | tf_op jit(solution)/shard_map/pallas_call | solution.py:776
